TPU v7x, 32 devices: a whole 2x2x4 slice. The times are simulated.
32 devices in a mesh: space: 8 (over z, y), nbr: 4 (over x, core).
Axes of the slice: x: 2, y: 2, z: 4, core: 2. Of those that a mesh axis runs over, the one named last changes fastest.
Arguments:
- nodes: bfloat16 [2, 3072, 512], P(None, 'space'), may hold values from -6 to 6
- edges: bfloat16 [2, 3072, 60, 192], P(None, 'space', 'nbr'), may hold values from -6 to 6
- neighbors: int32 [2, 3072, 60], P(None, 'space', 'nbr'), may hold values from 0 to 1215, as said below
- slot_live: int32 [2, 3072, 60], P(None, 'space', 'nbr'), may hold values from 0 to 1, as said below
- send_rows: int32 [2, 64, 8], P(None, 'space'), may hold values from 0 to 383
- message_self: bfloat16 [512, 512], replicated, may hold values from -0.25 to 0.25
- message_peer: bfloat16 [512, 512], replicated, may hold values from -0.25 to 0.25
- message_edge: bfloat16 [192, 512], replicated, may hold values from -0.4375 to 0.4375
- message_bias: bfloat16 [512], replicated, may hold values from -1.75 to 1.75
- message_out: bfloat16 [512, 512], replicated, may hold values from -0.25 to 0.25
- message_shift: bfloat16 [512], replicated, may hold values from -1.75 to 1.75
- first_gain: bfloat16 [512], replicated, may hold values from 0.5 to 1.5
- first_shift: bfloat16 [512], replicated, may hold values from -1.75 to 1.75
- hidden_in: bfloat16 [512, 2048], replicated, may hold values from -0.25 to 0.25
- hidden_bias: bfloat16 [2048], replicated, may hold values from -1.75 to 1.75
- hidden_out: bfloat16 [2048, 512], replicated, may hold values from -0.125 to 0.125
- output_bias: bfloat16 [512], replicated, may hold values from -1.75 to 1.75
- second_gain: bfloat16 [512], replicated, may hold values from 0.5 to 1.5
- second_shift: bfloat16 [512], replicated, may hold values from -1.75 to 1.75
- edge_self: bfloat16 [512, 192], replicated, may hold values from -0.25 to 0.25
- edge_peer: bfloat16 [512, 192], replicated, may hold values from -0.25 to 0.25
- edge_own: bfloat16 [192, 192], replicated, may hold values from -0.4375 to 0.4375
- edge_bias: bfloat16 [192], replicated, may hold values from -1.75 to 1.75
- edge_out: bfloat16 [192, 192], replicated, may hold values from -0.4375 to 0.4375
- edge_shift: bfloat16 [192], replicated, may hold values from -1.75 to 1.75
- third_gain: bfloat16 [192], replicated, may hold values from 0.5 to 1.5
- third_shift: bfloat16 [192], replicated, may hold values from -1.75 to 1.75
- node_cot: bfloat16 [2, 3072, 512], P(None, 'space'), may hold values from -6 to 6
- edge_cot: bfloat16 [2, 3072, 60, 192], P(None, 'space', 'nbr'), may hold values from -6 to 6
Outputs:
- new_nodes: bfloat16 [2, 3072, 512], P(None, 'space')
- new_edges: bfloat16 [2, 3072, 60, 192], P(None, 'space', 'nbr')
- node_grad: float32 [2, 3072, 512], P(None, 'space', 'nbr')
- edge_grad: bfloat16 [2, 3072, 60, 192], P(None, 'space', 'nbr')
- message_self_grad: float32 [512, 512], replicated
- message_peer_grad: float32 [512, 512], replicated
- message_edge_grad: float32 [192, 512], replicated
- message_bias_grad: float32 [512], replicated
- message_out_grad: float32 [512, 512], replicated
- message_shift_grad: float32 [512], replicated
- first_gain_grad: float32 [512], replicated
- first_shift_grad: float32 [512], replicated
- hidden_in_grad: float32 [512, 2048], replicated
- hidden_bias_grad: float32 [2048], replicated
- hidden_out_grad: float32 [2048, 512], replicated
- output_bias_grad: float32 [512], replicated
- second_gain_grad: float32 [512], replicated
- second_shift_grad: float32 [512], replicated
- edge_self_grad: float32 [512, 192], replicated
- edge_peer_grad: float32 [512, 192], replicated
- edge_own_grad: float32 [192, 192], replicated
- edge_bias_grad: float32 [192], replicated
- edge_out_grad: float32 [192, 192], replicated
- edge_shift_grad: float32 [192], replicated
- third_gain_grad: float32 [192], replicated
- third_shift_grad: float32 [192], replicated
Inputs may be any that keep to these rules, and one draw needn't show every extreme that they name: `neighbors`: A table index of residue i: below 1152 it names a row of the block before, the own block or the block after; from 1152 on it names an entry of the rows that the blocks send to i's block. The first block names no row before it, the last none after it. `slot_live`: the last rows of a block may be padding with no live slot; at least half of each block's rows are real residues. `send_rows`: row indices within the sending block.
All inputs are finite; a program needn't handle non-finite values.
Results may differ from a plain program's by a relative error of at most 0.017.
Values may be sent and summed in bfloat16 or wider, within the bound.
A program may use at most 320 MiB of HBM per device.

v0:
```python
import jax
import jax.numpy as jnp
from jax import lax
from jax.sharding import PartitionSpec as P

EPS = 1e-05
WIDE = jnp.float32
NARROW = jnp.bfloat16


def extended(cells, sides, width):
    for axis, dim in sides:
        count = lax.axis_size(axis)
        ends = count - 1
        head = lax.slice_in_dim(cells, 0, width, axis=dim)
        tail = lax.slice_in_dim(cells, cells.shape[dim] - width, cells.shape[dim], axis=dim)
        cells = jnp.concatenate(
            [
                lax.ppermute(tail, axis, [(i, (i + 1) % count) for i in range(ends)]),
                cells,
                lax.ppermute(head, axis, [((i + 1) % count, i) for i in range(ends)]),
            ],
            axis=dim,
        )
    return cells


def norm_apply(value, gain, shift):
    centre = value - jnp.mean(value, -1, keepdims=True)
    spread = jnp.mean(centre * centre, -1, keepdims=True)
    return centre * lax.rsqrt(spread + EPS) * gain + shift


def smooth(value):
    return jax.nn.gelu(value)


def product(left, right):
    return jnp.dot(left, right, preferred_element_type=WIDE)


def outer_sum(left, right):
    return lax.dot_general(left, right, (((0,), (0,)), ((), ())), preferred_element_type=WIDE)


def back_product(left, right):
    return lax.dot_general(left, right, (((1,), (1,)), ((), ())), preferred_element_type=WIDE)


def smooth_back(value, cotangent):
    return jax.vjp(smooth, value)[1](cotangent)[0]


def local(
    nodes,
    edges,
    neighbors,
    slot_live,
    send_rows,
    message_self,
    message_peer,
    message_edge,
    message_bias,
    message_out,
    message_shift,
    first_gain,
    first_shift,
    hidden_in,
    hidden_bias,
    hidden_out,
    output_bias,
    second_gain,
    second_shift,
    edge_self,
    edge_peer,
    edge_own,
    edge_bias,
    edge_out,
    edge_shift,
    third_gain,
    third_shift,
    node_cot,
    edge_cot,
):
    batches, block_rows, node_width = nodes.shape
    slot_count = edges.shape[2]
    edge_width = edges.shape[3]
    places = lax.axis_size("space")
    capacity = send_rows.shape[2]
    table_rows = 3 * block_rows + places * capacity
    edge_total = block_rows * slot_count
    lane_index = lax.axis_index("nbr")
    lane_width = node_width // lax.axis_size("nbr")
    weights = (
        message_self,
        message_peer,
        message_edge,
        message_bias,
        message_out,
        message_shift,
        first_gain,
        first_shift,
        hidden_in,
        hidden_bias,
        hidden_out,
        output_bias,
        second_gain,
        second_shift,
        edge_self,
        edge_peer,
        edge_own,
        edge_bias,
        edge_out,
        edge_shift,
        third_gain,
        third_shift,
    )
    running = [jnp.zeros(weight.shape, WIDE) for weight in weights]
    node_list = []
    edge_list = []
    node_grads = []
    edge_grads = []
    for sample in range(batches):
        rows_in = nodes[sample]
        edge_flat = edges[sample].reshape(edge_total, edge_width)
        index_flat = neighbors[sample].reshape(edge_total)
        live_slots = slot_live[sample].astype(WIDE)
        senders = send_rows[sample]
        send_flat = senders.reshape(places * capacity)
        self_term = product(rows_in, message_self)
        peer_term = product(rows_in, message_peer).astype(NARROW)
        peer_near = extended(peer_term, (("space", 0),), block_rows)
        peer_far = lax.all_to_all(
            peer_term[senders], "space", split_axis=0, concat_axis=0, tiled=True
        )
        peer_table = jnp.concatenate(
            [peer_near, peer_far.reshape(places * capacity, node_width)], 0
        )
        gathered = peer_table[index_flat].astype(WIDE)
        inner_slots = (
            gathered + product(edge_flat, message_edge) + message_bias.astype(WIDE)
        ).reshape(block_rows, slot_count, node_width) + self_term[:, None, :]
        inner_flat = inner_slots.reshape(edge_total, node_width)
        active = smooth(inner_flat).astype(NARROW)
        message = product(active, message_out) + message_shift.astype(WIDE)
        partial_value = jnp.sum(
            message.reshape(block_rows, slot_count, node_width) * live_slots[:, :, None], 1
        )
        counted = jnp.sum(live_slots, 1)
        summed, total_count = lax.psum((partial_value, counted), "nbr")
        cot_here = node_cot[sample]
        owner = (lane_index == 0).astype(WIDE)
        divisor = jnp.maximum(total_count, 1.0)[:, None]
        updated = rows_in.astype(WIDE) + summed / divisor
        node_hidden, first_back = jax.vjp(
            norm_apply, updated, first_gain.astype(WIDE), first_shift.astype(WIDE)
        )
        hidden_low = node_hidden.astype(NARROW)
        ffn_in = product(hidden_low, hidden_in) + hidden_bias.astype(WIDE)
        ffn_act = smooth(ffn_in).astype(NARROW)
        ffn_out = product(ffn_act, hidden_out) + output_bias.astype(WIDE)
        node_final, second_back = jax.vjp(
            norm_apply, node_hidden + ffn_out, second_gain.astype(WIDE), second_shift.astype(WIDE)
        )
        final_here = node_final.astype(NARROW)
        node_list.append(final_here)
        edge_self_term = product(final_here, edge_self)
        final_near = extended(final_here, (("space", 0),), block_rows)
        final_far = lax.all_to_all(
            final_here[senders], "space", split_axis=0, concat_axis=0, tiled=True
        )
        feature_table = jnp.concatenate(
            [final_near, final_far.reshape(places * capacity, node_width)], 0
        )
        edge_table = product(feature_table, edge_peer).astype(NARROW)
        edge_gathered = edge_table[index_flat].astype(WIDE)
        edge_inner = (
            edge_gathered + product(edge_flat, edge_own) + edge_bias.astype(WIDE)
        ).reshape(block_rows, slot_count, edge_width) + edge_self_term[:, None, :]
        edge_inner_flat = edge_inner.reshape(edge_total, edge_width)
        edge_active = smooth(edge_inner_flat).astype(NARROW)
        edge_update = product(edge_active, edge_out) + edge_shift.astype(WIDE)
        edge_final, third_back = jax.vjp(
            norm_apply,
            edge_flat.astype(WIDE) + edge_update,
            third_gain.astype(WIDE),
            third_shift.astype(WIDE),
        )
        edge_list.append(edge_final.astype(NARROW).reshape(block_rows, slot_count, edge_width))
        edge_sum_grad, third_gain_part, third_shift_part = third_back(
            edge_cot[sample].reshape(edge_total, edge_width).astype(WIDE)
        )
        update_low = edge_sum_grad.astype(NARROW)
        edge_shift_part = jnp.sum(update_low.astype(WIDE), 0)
        edge_out_part = outer_sum(edge_active, update_low)
        edge_inner_grad = smooth_back(edge_inner_flat, back_product(update_low, edge_out)).astype(
            NARROW
        )
        edge_bias_part = jnp.sum(edge_inner_grad.astype(WIDE), 0)
        edge_own_part = outer_sum(edge_flat, edge_inner_grad)
        edge_input_grad = edge_sum_grad + back_product(edge_inner_grad, edge_own)
        edge_inner_wide = edge_inner_grad.astype(WIDE)
        self_edge_grad = jnp.sum(
            edge_inner_wide.reshape(block_rows, slot_count, edge_width), 1
        ).astype(NARROW)
        edge_self_part = outer_sum(final_here, self_edge_grad)
        edge_table_grad = jax.ops.segment_sum(edge_inner_wide, index_flat, table_rows)
        edge_sides = jnp.concatenate(
            [edge_table_grad[:block_rows], edge_table_grad[2 * block_rows : 3 * block_rows]], 0
        )
        edge_back_near = extended(edge_sides, (("space", 0),), block_rows)
        edge_back_far = lax.all_to_all(
            edge_table_grad[3 * block_rows :].reshape(places, capacity, edge_width),
            "space",
            split_axis=0,
            concat_axis=0,
            tiled=True,
        )
        peer_edge_sum = (
            edge_table_grad[block_rows : 2 * block_rows]
            + edge_back_near[:block_rows]
            + edge_back_near[3 * block_rows :]
            + jax.ops.segment_sum(
                edge_back_far.reshape(places * capacity, edge_width), send_flat, block_rows
            )
        )
        peer_edge_low = peer_edge_sum.astype(NARROW)
        edge_peer_part = outer_sum(final_here, peer_edge_low)
        final_part = back_product(self_edge_grad, edge_self) + back_product(
            peer_edge_low, edge_peer
        )
        final_grad = cot_here.astype(WIDE) + lax.psum(final_part, "nbr")
        mid_grad, second_gain_part, second_shift_part = second_back(final_grad)
        ffn_out_low = mid_grad.astype(NARROW)
        output_bias_part = jnp.sum(ffn_out_low.astype(WIDE), 0)
        hidden_out_part = outer_sum(ffn_act, ffn_out_low)
        ffn_in_grad = smooth_back(ffn_in, back_product(ffn_out_low, hidden_out)).astype(NARROW)
        hidden_bias_part = jnp.sum(ffn_in_grad.astype(WIDE), 0)
        hidden_in_part = outer_sum(hidden_low, ffn_in_grad)
        hidden_grad = mid_grad + back_product(ffn_in_grad, hidden_in)
        updated_grad, first_gain_part, first_shift_part = first_back(hidden_grad)
        message_grad = (
            (live_slots[:, :, None] * (updated_grad / divisor)[:, None, :])
            .reshape(edge_total, node_width)
            .astype(NARROW)
        )
        message_shift_part = jnp.sum(message_grad.astype(WIDE), 0)
        message_out_part = outer_sum(active, message_grad)
        inner_grad = smooth_back(inner_flat, back_product(message_grad, message_out)).astype(NARROW)
        message_bias_part = jnp.sum(inner_grad.astype(WIDE), 0)
        message_edge_part = outer_sum(edge_flat, inner_grad)
        edge_input_grad = edge_input_grad + back_product(inner_grad, message_edge)
        inner_wide = inner_grad.astype(WIDE)
        self_node_grad = jnp.sum(inner_wide.reshape(block_rows, slot_count, node_width), 1).astype(
            NARROW
        )
        message_self_part = outer_sum(rows_in, self_node_grad)
        node_table_grad = jax.ops.segment_sum(inner_wide, index_flat, table_rows)
        node_sides = jnp.concatenate(
            [node_table_grad[:block_rows], node_table_grad[2 * block_rows : 3 * block_rows]], 0
        )
        node_back_near = extended(
            node_sides.astype(jnp.bfloat16), (("space", 0),), block_rows
        ).astype(node_sides.dtype)
        node_back_far = lax.all_to_all(
            node_table_grad[3 * block_rows :]
            .reshape(places, capacity, node_width)
            .astype(jnp.bfloat16),
            "space",
            split_axis=0,
            concat_axis=0,
            tiled=True,
        ).astype(jnp.float32)
        peer_node_sum = (
            node_table_grad[block_rows : 2 * block_rows]
            + node_back_near[:block_rows]
            + node_back_near[3 * block_rows :]
            + jax.ops.segment_sum(
                node_back_far.reshape(places * capacity, node_width), send_flat, block_rows
            )
        )
        peer_node_low = peer_node_sum.astype(NARROW)
        message_peer_part = outer_sum(rows_in, peer_node_low)
        rows_part = back_product(self_node_grad, message_self) + back_product(
            peer_node_low, message_peer
        )
        rows_share = lax.psum_scatter(
            rows_part.astype(jnp.bfloat16), "nbr", scatter_dimension=1, tiled=True
        ).astype(jnp.float32)
        node_grads.append(
            rows_share
            + lax.dynamic_slice_in_dim(updated_grad, lane_index * lane_width, lane_width, 1)
        )
        edge_grads.append(
            edge_input_grad.astype(NARROW).reshape(block_rows, slot_count, edge_width)
        )
        fresh = (
            message_self_part,
            message_peer_part,
            message_edge_part,
            message_bias_part,
            message_out_part,
            message_shift_part,
            first_gain_part * owner,
            first_shift_part * owner,
            hidden_in_part * owner,
            hidden_bias_part * owner,
            hidden_out_part * owner,
            output_bias_part * owner,
            second_gain_part * owner,
            second_shift_part * owner,
            edge_self_part,
            edge_peer_part,
            edge_own_part,
            edge_bias_part,
            edge_out_part,
            edge_shift_part,
            third_gain_part,
            third_shift_part,
        )
        running = [earlier + latest for earlier, latest in zip(running, fresh)]
    reduced = lax.psum(
        (
            running[0],
            running[1],
            running[2],
            running[3],
            running[4],
            running[5],
            running[6],
            running[7],
            running[8],
            running[9],
            running[10],
            running[11],
            running[12],
            running[13],
            running[14],
            running[15],
            running[16],
            running[17],
            running[18],
            running[19],
            running[20],
            running[21],
        ),
        ("space", "nbr"),
    )
    return (
        jnp.stack(node_list),
        jnp.stack(edge_list),
        jnp.stack(node_grads),
        jnp.stack(edge_grads),
        reduced[0],
        reduced[1],
        reduced[2],
        reduced[3],
        reduced[4],
        reduced[5],
        reduced[6],
        reduced[7],
        reduced[8],
        reduced[9],
        reduced[10],
        reduced[11],
        reduced[12],
        reduced[13],
        reduced[14],
        reduced[15],
        reduced[16],
        reduced[17],
        reduced[18],
        reduced[19],
        reduced[20],
        reduced[21],
    )


def solution(mesh):
    return jax.shard_map(
        local,
        mesh=mesh,
        in_specs=(
            P(None, "space", None),
            P(None, "space", "nbr", None),
            P(None, "space", "nbr"),
            P(None, "space", "nbr"),
            P(None, "space", None),
            P(),
            P(),
            P(),
            P(),
            P(),
            P(),
            P(),
            P(),
            P(),
            P(),
            P(),
            P(),
            P(),
            P(),
            P(),
            P(),
            P(),
            P(),
            P(),
            P(),
            P(),
            P(),
            P(None, "space", None),
            P(None, "space", "nbr", None),
        ),
        out_specs=(
            P(None, "space", None),
            P(None, "space", "nbr", None),
            P(None, "space", "nbr"),
            P(None, "space", "nbr", None),
            P(),
            P(),
            P(),
            P(),
            P(),
            P(),
            P(),
            P(),
            P(),
            P(),
            P(),
            P(),
            P(),
            P(),
            P(),
            P(),
            P(),
            P(),
            P(),
            P(),
            P(),
            P(),
        ),
        check_vma=False,
    )
```

profile of v0, /device:TPU:0, one launch (start us, length us, event | category | flops | bytes accessed | tf_op | source)
XLA Modules:
  0.0 1312.9 jit_solution(12360364182696285249)
XLA Ops:
  54.5 7.1 slice_convert_fusion
  105.3 12.5 add.596
  124.1 12.5 add.621
  144.8 17.4 %gather_fusion.3 = bf16[5760,512]{1,0:T(8,128)(2,1)} fusion(bf16[1216,512]{1,0:T(8,128)(2,1)S(1)} %pad_maximum_fusion.3, s32[6144]{0:T(1024)} %pad_clamp_fusion), kind=kCustom, calls=%fused_computation.3 | custom fusion | bytes 11819520 | tf_op jit(solution)/shard_map/gather | solution.py:139
  163.5 17.4 %gather_fusion.1 = bf16[5760,512]{1,0:T(8,128)(2,1)} fusion(bf16[1216,512]{1,0:T(8,128)(2,1)S(1)} %pad_maximum_fusion.2, s32[6144]{0:T(1024)} %pad_clamp_fusion.1), kind=kCustom, calls=%fused_computation.1 | custom fusion | bytes 11819520 | tf_op jit(solution)/shard_map/gather | solution.py:139
  181.0 26.0 %multiply_convert_fusion.5 = (bf16[5760,512]{1,0:T(8,128)(2,1)}, bf16[5760,512]{1,0:T(8,128)(2,1)}, f32[5760,512]{1,0:T(8,128)}) fusion(f32[5760,512]{1,0:T(8,128)} %add.596, f32[512]{0:T(512)} %convert_element_type.329, bf16[5760,512]{1,0:T(8,128)(2,1)} %gather_fusion.1, f32[5760,512]{1,0:T(8,128)} %add.621, f32[5760,512]{1,0:T(8,128)} %fusion.193, ...), kind=kOutput, calls=%fused_computation.44 | convolution fusion | flops 1209139200 | bytes 73189376 | tf_op jit(solution)/shard_map/dot_general | solution.py:39
  207.0 8.8 convolution_add_fusion.1
  215.7 12.5 reshape.477
  228.2 8.7 convolution_add_fusion
  236.9 12.5 reshape.479
  249.4 8.0 multiply_reduce_fusion.1
  264.4 7.0 copy.140
  271.5 7.1 reshape.499
  284.6 6.6 copy.134
  291.2 7.1 reshape.495
  347.8 7.1 add.653
  365.0 7.1 add.640
  395.1 17.4 %gather_fusion.7 = bf16[5760,192]{1,0:T(8,128)(2,1)} fusion(bf16[1216,192]{1,0:T(8,128)(2,1)S(1)} %copy.128, s32[6144]{0:T(1024)} %pad_clamp_fusion), kind=kCustom, calls=%fused_computation.7 | custom fusion | bytes 4446720 | tf_op jit(solution)/shard_map/gather | solution.py:176
  416.8 17.2 %gather_fusion.5 = bf16[5760,192]{1,0:T(8,128)(2,1)} fusion(bf16[1216,192]{1,0:T(8,128)(2,1)S(1)} %copy.122, s32[6144]{0:T(1024)S(1)} %copy-done.71), kind=kCustom, calls=%fused_computation.5 | custom fusion | bytes 4446720 | tf_op jit(solution)/shard_map/gather | solution.py:176
  462.0 7.7 fusion.178
  486.7 7.1 reshape.482
  493.8 31.0 %scatter_custom_fusion = f32[1216,192]{1,0:T(8,128)S(1)} fusion(s32[5760]{0:T(1024)} %reshape.568, f32[5760,192]{1,0:T(8,128)} %copy.136, f32[]{:T(128)} %constant.74.clone.1), kind=kCustom, calls=%fused_computation.221 | custom fusion | flops 1105920 | bytes 934400 | tf_op jit(solution)/shard_map/scatter-add | solution.py:207
  530.5 7.6 convert_reduce_fusion.8
  566.1 31.8 %scatter_custom_fusion.4 = f32[1216,192]{1,0:T(8,128)} fusion(s32[5760]{0:T(1024)} %reshape.600, f32[5760,192]{1,0:T(8,128)} %copy.142, f32[]{:T(128)} %constant.74.clone.1), kind=kCustom, calls=%fused_computation.219 | custom fusion | flops 1105920 | bytes 934400 | tf_op jit(solution)/shard_map/scatter-add | solution.py:207
  601.3 7.1 reshape.488
  623.9 6.8 all-to-all-start.6
  646.2 40.0 %all-reduce.11.cloned.1.call-done = (f32[384,512]{1,0:T(8,128)}, f32[384,512]{1,0:T(8,128)}) async-done(((f32[384,512]{1,0:T(8,128)}, f32[384,512]{1,0:T(8,128)}), (f32[384,512]{1,0:T(8,128)}, f32[384,512]{1,0:T(8,128)})) %all-reduce.11.cloned.1.call-update) | async-done | bytes 1572880 | tf_op jit(solution)/shard_map/psum | solution.py:232
  718.4 12.7 mul.795
  731.1 10.5 fusion.165
  741.7 18.0 %convert_reduce_fusion.3 = (f32[512]{0:T(512)S(1)}, bf16[5760,512]{1,0:T(8,128)(2,1)}) fusion(f32[5760,512]{1,0:T(8,128)} %add.596, f32[512]{0:T(512)S(1)} %copy-done.134, f32[5760,512]{1,0:T(8,128)} %get-tuple-element.233, bf16[5760,512]{1,0:T(8,128)(2,1)} %gather_fusion.1, bf16[512,512]{1,0:T(8,128)(2,1)S(1)} %copy-done.155, ...), kind=kOutput, calls=%fused_computation.75 | convolution fusion | flops 3102473728 | bytes 47737344 | tf_op jit(solution)/shard_map/dot_general | solution.py:47
  759.7 39.4 %scatter_custom_fusion.2 = f32[1216,512]{1,0:T(8,128)} fusion(s32[5760]{0:T(1024)} %reshape.568, bf16[5760,512]{1,0:T(8,128)(2,1)} %get-tuple-element.246, f32[]{:T(128)} %constant.74.clone.1), kind=kCustom, calls=%fused_computation.76 | custom fusion | flops 5898240 | bytes 8389120 | tf_op jit(solution)/shard_map/scatter-add | solution.py:258
  802.5 10.0 reshape.485
  812.6 7.7 reduce_sum.531
  825.3 6.3 mul.845
  831.5 12.5 mul.846
  844.0 21.2 %convert_reduce_fusion.2 = (f32[512]{0:T(512)S(1)}, bf16[5760,512]{1,0:T(8,128)(2,1)S(1)}) fusion(f32[5760,512]{1,0:T(8,128)} %add.621, f32[512]{0:T(512)S(1)} %copy-done.134, f32[5760,512]{1,0:T(8,128)} %fusion.193, bf16[5760,512]{1,0:T(8,128)(2,1)} %gather_fusion.3, bf16[512,512]{1,0:T(8,128)(2,1)} %param.38, f32[5760,512]{1,0:T(8,128)} %mul.846, ...), kind=kOutput, calls=%fused_computation.72 | convolution fusion | flops 3102473728 | bytes 47737344 | tf_op jit(solution)/shard_map/dot_general | solution.py:47
  869.1 39.5 %scatter_custom_fusion.6 = f32[1216,512]{1,0:T(8,128)} fusion(s32[5760]{0:T(1024)} %reshape.600, bf16[5760,512]{1,0:T(8,128)(2,1)} %copy-done.4, f32[]{:T(128)} %constant.74.clone.1), kind=kCustom, calls=%fused_computation.73 | custom fusion | flops 5898240 | bytes 8389120 | tf_op jit(solution)/shard_map/scatter-add | solution.py:258
  912.1 9.6 reshape.491
  933.5 11.3 convolution_add_fusion.12
  953.0 7.7 reduce_sum.545
  960.7 7.1 add_multiply_fusion
  972.8 6.7 all-to-all-start.7
  1024.2 7.0 pad_maximum_fusion
  1031.2 8.6 copy.149
  1075.0 7.1 pad_maximum_fusion.1
  1082.2 8.8 copy.150
  1093.9 41.5 %all-reduce = (f32[512]{0:T(512)}, f32[512]{0:T(512)}, f32[512]{0:T(512)}, f32[512]{0:T(512)}, f32[2048]{0:T(1024)}, /*index=5*/f32[512]{0:T(512)}, f32[512]{0:T...) all-reduce(f32[512]{0:T(512)S(1)} %add.690, ...), channel_id=1, replica_groups=mesh['space'=8,'nbr'=4] {'space','nbr'}, use_global_device_ids=true, to_apply=%region_53.0 | all-reduce | flops 6400 | bytes 51200 | tf_op jit(solution)/shard_map/psum | solution.py:322
  1140.1 148.1 %all-reduce.9.cloned.1.call-done = (f32[512,512]{0,1:T(8,128)}, f32[512,512]{0,1:T(8,128)}, f32[192,512]{1,0:T(8,128)}, f32[512,512]{1,0:T(8,128)}, f32[512,2048...) async-done(((f32[512,512]{0,1:T(8,128)}, f32[512,512]{0,1:T(8,128)}, ...) | async-done | bytes 13008912 | tf_op jit(solution)/shard_map/psum | solution.py:322
  (655 shorter events, 496.1 us)
Async XLA Ops:
  7.2 307.4 %copy-start = (bf16[2048,512]{1,0:T(8,128)(2,1)S(1)}, bf16[2048,512]{1,0:T(8,128)(2,1)}, u32[]{:S(2)}) copy-start(bf16[2048,512]{1,0:T(8,128)(2,1)} %param.44) | copy-start | bytes 6291460
  7.2 30.1 %copy-start.25 = (bf16[2,384,512]{2,1,0:T(8,128)(2,1)S(1)}, bf16[2,384,512]{2,1,0:T(8,128)(2,1)}, u32[]{:S(2)}) copy-start(bf16[2,384,512]{2,1,0:T(8,128)(2,1)} %param.29) | copy-start | bytes 2359300
  7.2 30.1 %copy-start.33 = (bf16[512,512]{1,0:T(8,128)(2,1)S(1)}, bf16[512,512]{1,0:T(8,128)(2,1)}, u32[]{:S(2)}) copy-start(bf16[512,512]{1,0:T(8,128)(2,1)} %param.34) | copy-start | bytes 1572868
  7.2 31.4 %copy-start.83 = (s32[2,384,15]{1,0,2:T(2,128)S(1)}, s32[2,384,15]{1,0,2:T(2,128)}, u32[]{:S(2)}) copy-start(s32[2,384,15]{1,0,2:T(2,128)} %param.31) | copy-start | bytes 138244
  7.3 31.4 %copy-start.84 = (s32[2,384,15]{1,0,2:T(2,128)S(1)}, s32[2,384,15]{1,0,2:T(2,128)}, u32[]{:S(2)}) copy-start(s32[2,384,15]{1,0,2:T(2,128)} %param.32) | copy-start | bytes 138244
  9.7 152.5 %collective-permute-start.1 = (bf16[384,512]{1,0:T(8,128)(2,1)}, bf16[384,512]{1,0:T(8,128)(2,1)}, u32[]{:S(2)}, u32[]{:S(2)}) collective-permute-start(bf16[384,512]{1,0:T(8,128)(2,1)} %convolution_convert_fusion.3), channel_id=1, source_target_pairs={{4,0},{8,4},{12,8},{16,12},{20,16},{24,20},{28,24},{5,1},{9,5},{13... | collective-permute-start | bytes 1179656 | tf_op jit(solution)/shard_map/ppermute | solution.py:21
  11.0 151.2 %collective-permute-start = (bf16[384,512]{1,0:T(8,128)(2,1)}, bf16[384,512]{1,0:T(8,128)(2,1)}, u32[]{:S(2)}, u32[]{:S(2)}) collective-permute-start(bf16[384,512]{1,0:T(8,128)(2,1)} %convolution_convert_fusion.3), channel_id=1, source_target_pairs={{0,4},{4,8},{8,12},{12,16},{16,20},{20,24},{24,28},{1,5},{5,9},{9,... | collective-permute-start | bytes 1179656 | tf_op jit(solution)/shard_map/ppermute | solution.py:19
  19.5 123.9 %collective-permute-start.3 = (bf16[384,512]{1,0:T(8,128)(2,1)}, bf16[384,512]{1,0:T(8,128)(2,1)}, u32[]{:S(2)}, u32[]{:S(2)}) collective-permute-start(bf16[384,512]{1,0:T(8,128)(2,1)} %convolution_convert_fusion.2), channel_id=1, source_target_pairs={{4,0},{8,4},{12,8},{16,12},{20,16},{24,20},{28,24},{5,1},{9,5},{13... | collective-permute-start | bytes 1179656 | tf_op jit(solution)/shard_map/ppermute | solution.py:21
  20.8 122.6 %collective-permute-start.2 = (bf16[384,512]{1,0:T(8,128)(2,1)}, bf16[384,512]{1,0:T(8,128)(2,1)}, u32[]{:S(2)}, u32[]{:S(2)}) collective-permute-start(bf16[384,512]{1,0:T(8,128)(2,1)} %convolution_convert_fusion.2), channel_id=1, source_target_pairs={{0,4},{4,8},{8,12},{12,16},{16,20},{20,24},{24,28},{1,5},{5,9},{9,... | collective-permute-start | bytes 1179656 | tf_op jit(solution)/shard_map/ppermute | solution.py:19
  29.5 107.7 %all-to-all-start.1 = ((bf16[8,8,512]{2,1,0:T(8,128)(2,1)}), bf16[8,8,512]{2,1,0:T(8,128)(2,1)}, u32[]{:S(2)}, u32[]{:S(2)}) async-start(bf16[8,8,512]{2,1,0:T(8,128)(2,1)} %bitcast.8), calls=%async_computation.1 | async-start | bytes 131072 | tf_op jit(solution)/shard_map/all_to_all | solution.py:133
  80.7 232.8 %copy-start.125 = (f32[2048]{0:T(1024)}, f32[2048]{0:T(1024)S(1)}, u32[]{:S(2)}) copy-start(f32[2048]{0:T(1024)S(1)} %convert_element_type.337) | copy-start | bytes 24580
  81.6 167.7 %copy-start.51 = (f32[384,15]{1,0:T(8,128)}, f32[384,15]{1,0:T(8,128)S(1)}, u32[]{:S(2)}) copy-start(f32[384,15]{1,0:T(8,128)S(1)} %copy.116) | copy-start | bytes 69124
  137.2 25.0 %all-to-all-start = ((bf16[8,8,512]{2,1,0:T(8,128)(2,1)}), bf16[8,8,512]{2,1,0:T(8,128)(2,1)}, u32[]{:S(2)}, u32[]{:S(2)}) async-start(bf16[8,8,512]{2,1,0:T(8,128)(2,1)} %bitcast.2), calls=%async_computation | async-start | bytes 131072 | tf_op jit(solution)/shard_map/all_to_all | solution.py:133
  143.2 167.0 %all-reduce.13.cloned.1.call-start = ((), (), s32[]{:S(2)}) async-start(), calls=%async_computation.14 | async-start | bytes 3145728 | tf_op jit(solution)/shard_map/psum | solution.py:150
  181.0 26.0 %copy-start.136 = (f32[512]{0:T(512)S(1)}, f32[512]{0:T(512)}, u32[]{:S(2)}) copy-start(f32[512]{0:T(512)} %convert_element_type.331) | copy-start | bytes 6148
  181.0 26.0 %copy-start.154 = (bf16[512,512]{1,0:T(8,128)(2,1)S(1)}, bf16[512,512]{1,0:T(8,128)(2,1)}, u32[]{:S(2)}) copy-start(bf16[512,512]{1,0:T(8,128)(2,1)} %param.38) | copy-start | bytes 1572868
  319.3 23.0 %copy-start.86 = (s32[1024]{0:T(1024)S(1)}, s32[1024]{0:T(1024)}, u32[]{:S(2)}) copy-start(s32[1024]{0:T(1024)} %copy-done.85) | copy-start | bytes 12292
  320.3 64.1 %copy-start.11 = (bf16[384,512]{1,0:T(8,128)(2,1)}, bf16[384,512]{1,0:T(8,128)(2,1)S(1)}, u32[]{:S(2)}) copy-start(bf16[384,512]{1,0:T(8,128)(2,1)S(1)} %get-tuple-element.219) | copy-start | bytes 1179652
  320.3 71.0 %copy-start.14 = (bf16[384,512]{1,0:T(8,128)(2,1)}, bf16[384,512]{1,0:T(8,128)(2,1)S(1)}, u32[]{:S(2)}) copy-start(bf16[384,512]{1,0:T(8,128)(2,1)S(1)} %get-tuple-element.220) | copy-start | bytes 1179652
  321.6 62.7 %collective-permute-start.5 = (bf16[384,512]{1,0:T(8,128)(2,1)S(1)}, bf16[384,512]{1,0:T(8,128)(2,1)}, u32[]{:S(2)}, u32[]{:S(2)}) collective-permute-start(bf16[384,512]{1,0:T(8,128)(2,1)S(1)} %get-tuple-element.219), channel_id=1, source_target_pairs={{4,0},{8,4},{12,8},{16,12},{20,16},{24,20},{28,24},{5,1},{9,5},{13... | collective-permute-start | bytes 1179656 | tf_op jit(solution)/shard_map/ppermute | solution.py:21
  322.9 61.5 %collective-permute-start.4 = (bf16[384,512]{1,0:T(8,128)(2,1)S(1)}, bf16[384,512]{1,0:T(8,128)(2,1)}, u32[]{:S(2)}, u32[]{:S(2)}) collective-permute-start(bf16[384,512]{1,0:T(8,128)(2,1)S(1)} %get-tuple-element.219), channel_id=1, source_target_pairs={{0,4},{4,8},{8,12},{12,16},{16,20},{20,24},{24,28},{1,5},{5,9},{9,... | collective-permute-start | bytes 1179656 | tf_op jit(solution)/shard_map/ppermute | solution.py:19
  328.2 63.1 %collective-permute-start.7 = (bf16[384,512]{1,0:T(8,128)(2,1)S(1)}, bf16[384,512]{1,0:T(8,128)(2,1)}, u32[]{:S(2)}, u32[]{:S(2)}) collective-permute-start(bf16[384,512]{1,0:T(8,128)(2,1)S(1)} %get-tuple-element.220), channel_id=1, source_target_pairs={{4,0},{8,4},{12,8},{16,12},{20,16},{24,20},{28,24},{5,1},{9,5},{13... | collective-permute-start | bytes 1179656 | tf_op jit(solution)/shard_map/ppermute | solution.py:21
  329.5 61.8 %collective-permute-start.6 = (bf16[384,512]{1,0:T(8,128)(2,1)S(1)}, bf16[384,512]{1,0:T(8,128)(2,1)}, u32[]{:S(2)}, u32[]{:S(2)}) collective-permute-start(bf16[384,512]{1,0:T(8,128)(2,1)S(1)} %get-tuple-element.220), channel_id=1, source_target_pairs={{0,4},{4,8},{8,12},{12,16},{16,20},{20,24},{24,28},{1,5},{5,9},{9,... | collective-permute-start | bytes 1179656 | tf_op jit(solution)/shard_map/ppermute | solution.py:19
  335.0 43.1 %all-to-all-start.2 = ((bf16[8,8,512]{2,1,0:T(8,128)(2,1)}), bf16[8,8,512]{2,1,0:T(8,128)(2,1)S(1)}, u32[]{:S(2)}, u32[]{:S(2)}) async-start(bf16[8,8,512]{2,1,0:T(8,128)(2,1)} %bitcast.12), calls=%async_computation.2 | async-start | bytes 131072 | tf_op jit(solution)/shard_map/all_to_all | solution.py:169
  378.1 13.2 %all-to-all-start.3 = ((bf16[8,8,512]{2,1,0:T(8,128)(2,1)}), bf16[8,8,512]{2,1,0:T(8,128)(2,1)}, u32[]{:S(2)}, u32[]{:S(2)}) async-start(bf16[8,8,512]{2,1,0:T(8,128)(2,1)} %bitcast.14), calls=%async_computation.3 | async-start | bytes 131072 | tf_op jit(solution)/shard_map/all_to_all | solution.py:169
  549.3 74.6 %all-to-all-start.4 = ((f32[8,8,192]{2,1,0:T(8,128)}), f32[8,8,192]{2,1,0:T(8,128)}, u32[]{:S(2)}, u32[]{:S(2)}) async-start(f32[8,8,192]{2,1,0:T(8,128)} %slice_bitcast_fusion.3), calls=%async_computation.4 | async-start | bytes 131072 | tf_op jit(solution)/shard_map/all_to_all | solution.py:212
  560.2 61.7 %collective-permute-start.8 = (f32[384,192]{1,0:T(8,128)}, f32[384,192]{1,0:T(8,128)}, u32[]{:S(2)}, u32[]{:S(2)}) collective-permute-start(f32[384,192]{1,0:T(8,128)} %get-tuple-element.201), channel_id=1, source_target_pairs={{0,4},{4,8},{8,12},{12,16},{16,20},{20,24},{24,28},{1,5},{5,9},{9,... | collective-permute-start | bytes 884744 | tf_op jit(solution)/shard_map/ppermute | solution.py:19
  564.8 57.2 %collective-permute-start.9 = (f32[384,192]{1,0:T(8,128)}, f32[384,192]{1,0:T(8,128)}, u32[]{:S(2)}, u32[]{:S(2)}) collective-permute-start(f32[384,192]{1,0:T(8,128)} %get-tuple-element.202), channel_id=1, source_target_pairs={{4,0},{8,4},{12,8},{16,12},{20,16},{24,20},{28,24},{5,1},{9,5},{13... | collective-permute-start | bytes 884744 | tf_op jit(solution)/shard_map/ppermute | solution.py:21
  613.3 23.1 %collective-permute-start.12 = (f32[384,192]{1,0:T(8,128)}, f32[384,192]{1,0:T(8,128)}, u32[]{:S(2)}, u32[]{:S(2)}) collective-permute-start(f32[384,192]{1,0:T(8,128)} %get-tuple-element.199), channel_id=1, source_target_pairs={{0,4},{4,8},{8,12},{12,16},{16,20},{20,24},{24,28},{1,5},{5,9},{9,... | collective-permute-start | bytes 884744 | tf_op jit(solution)/shard_map/ppermute | solution.py:19
  618.6 17.8 %collective-permute-start.13 = (f32[384,192]{1,0:T(8,128)}, f32[384,192]{1,0:T(8,128)}, u32[]{:S(2)}, u32[]{:S(2)}) collective-permute-start(f32[384,192]{1,0:T(8,128)} %get-tuple-element.200), channel_id=1, source_target_pairs={{4,0},{8,4},{12,8},{16,12},{20,16},{24,20},{28,24},{5,1},{9,5},{13... | collective-permute-start | bytes 884744 | tf_op jit(solution)/shard_map/ppermute | solution.py:21
  623.9 13.8 %all-to-all-start.6 = ((f32[8,8,192]{2,1,0:T(8,128)}), f32[8,8,192]{2,1,0:T(8,128)S(1)}, u32[]{:S(2)}, u32[]{:S(2)}) async-start(f32[8,8,192]{2,1,0:T(8,128)} %slice_bitcast_fusion.1), calls=%async_computation.6 | async-start | bytes 131072 | tf_op jit(solution)/shard_map/all_to_all | solution.py:212
  630.7 55.5 %all-reduce.11.cloned.1.call-start = ((), (), s32[]{:S(2)}) async-start(), calls=%async_computation.13 | async-start | bytes 3145728 | tf_op jit(solution)/shard_map/psum | solution.py:232
  638.9 47.3 %copy-start.90 = (f32[512]{0:T(512)S(1)}, f32[512]{0:T(512)}, u32[]{:S(2)}) copy-start(f32[512]{0:T(512)} %convert_element_type.340) | copy-start | bytes 6148
  638.9 47.3 %copy-start.92 = (f32[384]{0:T(512)S(1)}, f32[384]{0:T(512)}, u32[]{:S(2)}) copy-start(f32[384]{0:T(512)} %copy-done.91) | copy-start | bytes 4612
  639.0 47.3 %copy-start.94 = (f32[384]{0:T(512)S(1)}, f32[384]{0:T(512)}, u32[]{:S(2)}) copy-start(f32[384]{0:T(512)} %copy-done.93) | copy-start | bytes 4612
  641.4 48.4 %copy-start.115 = (f32[384]{0:T(512)S(1)}, f32[384]{0:T(512)}, u32[]{:S(2)}) copy-start(f32[384]{0:T(512)} %copy-done.114) | copy-start | bytes 4612
  641.4 48.4 %copy-start.113 = (f32[384]{0:T(512)S(1)}, f32[384]{0:T(512)}, u32[]{:S(2)}) copy-start(f32[384]{0:T(512)} %copy-done.112) | copy-start | bytes 4612
  644.0 45.8 %copy-start.18 = (f32[384,512]{1,0:T(8,128)S(1)}, f32[384,512]{1,0:T(8,128)}, u32[]{:S(2)}) copy-start(f32[384,512]{1,0:T(8,128)} %copy-done.17) | copy-start | bytes 2359300
  844.0 23.7 %copy-start.3 = (bf16[5760,192]{1,0:T(8,128)(2,1)S(1)}, bf16[5760,192]{1,0:T(8,128)(2,1)}, u32[]{:S(2)}) copy-start(bf16[5760,192]{1,0:T(8,128)(2,1)} %reshape_squeeze.17) | copy-start | bytes 6635524
  921.7 51.1 %all-to-all-start.5 = ((bf16[8,8,512]{2,1,0:T(8,128)(2,1)}), bf16[8,8,512]{2,1,0:T(8,128)(2,1)S(1)}, u32[]{:S(2)}, u32[]{:S(2)}) async-start(bf16[8,8,512]{2,1,0:T(8,128)(2,1)} %slice_bitcast_fusion.2), calls=%async_computation.5 | async-start | bytes 131072 | tf_op jit(solution)/shard_map/all_to_all | solution.py:265
  927.2 44.1 %collective-permute-start.10 = (bf16[384,512]{1,0:T(8,128)(2,1)}, bf16[384,512]{1,0:T(8,128)(2,1)}, u32[]{:S(2)}, u32[]{:S(2)}) collective-permute-start(bf16[384,512]{1,0:T(8,128)(2,1)} %get-tuple-element.195), channel_id=1, source_target_pairs={{0,4},{4,8},{8,12},{12,16},{16,20},{20,24},{24,28},{1,5},{5,9},{9,... | collective-permute-start | bytes 1179656 | tf_op jit(solution)/shard_map/ppermute | solution.py:19
  931.9 39.4 %collective-permute-start.11 = (bf16[384,512]{1,0:T(8,128)(2,1)}, bf16[384,512]{1,0:T(8,128)(2,1)}, u32[]{:S(2)}, u32[]{:S(2)}) collective-permute-start(bf16[384,512]{1,0:T(8,128)(2,1)} %get-tuple-element.196), channel_id=1, source_target_pairs={{4,0},{8,4},{12,8},{16,12},{20,16},{24,20},{28,24},{5,1},{9,5},{13... | collective-permute-start | bytes 1179656 | tf_op jit(solution)/shard_map/ppermute | solution.py:21
  946.9 39.8 %collective-permute-start.14 = (bf16[384,512]{1,0:T(8,128)(2,1)}, bf16[384,512]{1,0:T(8,128)(2,1)}, u32[]{:S(2)}, u32[]{:S(2)}) collective-permute-start(bf16[384,512]{1,0:T(8,128)(2,1)} %get-tuple-element.197), channel_id=1, source_target_pairs={{0,4},{4,8},{8,12},{12,16},{16,20},{20,24},{24,28},{1,5},{5,9},{9,... | collective-permute-start | bytes 1179656 | tf_op jit(solution)/shard_map/ppermute | solution.py:19
  951.5 35.2 %collective-permute-start.15 = (bf16[384,512]{1,0:T(8,128)(2,1)}, bf16[384,512]{1,0:T(8,128)(2,1)}, u32[]{:S(2)}, u32[]{:S(2)}) collective-permute-start(bf16[384,512]{1,0:T(8,128)(2,1)} %get-tuple-element.198), channel_id=1, source_target_pairs={{4,0},{8,4},{12,8},{16,12},{20,16},{24,20},{28,24},{5,1},{9,5},{13... | collective-permute-start | bytes 1179656 | tf_op jit(solution)/shard_map/ppermute | solution.py:21
  972.8 16.2 %all-to-all-start.7 = ((bf16[8,8,512]{2,1,0:T(8,128)(2,1)}), bf16[8,8,512]{2,1,0:T(8,128)(2,1)S(1)}, u32[]{:S(2)}, u32[]{:S(2)}) async-start(bf16[8,8,512]{2,1,0:T(8,128)(2,1)} %slice_bitcast_fusion), calls=%async_computation.7 | async-start | bytes 131072 | tf_op jit(solution)/shard_map/all_to_all | solution.py:265
  979.5 155.9 %reduce-scatter.7.cloned.1.call-start = ((), (), s32[]{:S(2)}) async-start(), calls=%async_computation.10 | async-start | bytes 491520
  985.3 151.1 %reduce-scatter.9.cloned.1.call-start = ((), (), s32[]{:S(2)}) async-start(), calls=%async_computation.11 | async-start | bytes 491520
  995.1 293.2 %all-reduce.9.cloned.1.call-start = ((), (), s32[]{:S(2)}) async-start(), calls=%async_computation.12 | async-start | bytes 26214400 | tf_op jit(solution)/shard_map/psum | solution.py:322
  (162 other events, 1149.2 us)
Sparse Core Ops, SparseCore 0:
  261.4 44.4 all-reduce.12
  641.5 44.6 all-reduce.10
  985.5 21.2 reduce-scatter.6
  1009.7 20.7 reduce-scatter.8
  1038.0 250.1 all-reduce.8
where the time goes:
time: 1330 us; the launch traced here: 1310 us
  local copies, waits for them, and re-layouts  452 us (34%)
  other arithmetic  271 us (20%)
  matrix products  236 us (18%)
  waiting for transfers between devices  191 us (14%)
  starting transfers between devices  98.7 us (7%)
  blocking collectives  47.1 us (4%)
  between operations  16.5 us (1%)
    psum x1, waiting for transfers between devices, local(): lax.psum((running[0], running[1], running[2], running[3], running[4], run...  148 us
    dot_general x20, matrix products, back_product(): lax.dot_general(left, right, (((1,), (1,)), ((), ())), preferred_element_...  91.5 us
    dot_general x20, matrix products, product(): return jnp.dot(left, right, preferred_element_type=WIDE)  81.8 us
    scatter-add x2, other arithmetic, local(): node_table_grad = jax.ops.segment_sum(inner_wide, index_flat, table_rows)  78.9 us
    dot_general x20, matrix products, outer_sum(): lax.dot_general(left, right, (((0,), (0,)), ((), ())), preferred_element_...  62.8 us
    scatter-add x2, other arithmetic, local(): jax.ops.segment_sum(edge_inner_wide, index_flat, table_rows)  62.7 us
    unnamed x378, local copies, waits for them, and re-layouts  55.3 us
    gather x4, local copies, waits for them, and re-layouts, local(): edge_gathered = edge_table[index_flat].astype(WIDE)  43.4 us
  transfers between devices with their start and end apart: 29, of which 3 were waited for; matrix products, arithmetic and copies ran while one was open for 33% of the time, Pallas kernels for 0%

commit v1 on v0

v1 whole, which is shorter than its diff:
```python
import itertools
from types import SimpleNamespace

import jax
import jax.numpy as jnp
from jax import lax
from jax.experimental import pallas as pl
from jax.experimental.pallas import tpu as pltpu
from jax.sharding import PartitionSpec as P

EPS = 1e-05
F32 = jnp.float32
BF = jnp.bfloat16
MESH = pl.DeviceIdType.MESH
VMEM_LIMIT = 62 << 20
C0 = 0.7978845608028654
C1 = C0 * 0.044715
GROUP = 3
LANES = 128
SPLITS = 5


def dot(left, right):
    return jnp.dot(left, right, preferred_element_type=F32)


def dot_nt(left, right):
    return lax.dot_general(left, right, (((1,), (1,)), ((), ())), preferred_element_type=F32)


def dot_tn(left, right):
    return lax.dot_general(left, right, (((0,), (0,)), ((), ())), preferred_element_type=F32)


def gelu_both(x):
    x2 = x * x
    half = 0.5 * jnp.tanh(x * (C0 + C1 * x2)) + 0.5
    act = x * half
    return act, half + act * (1.0 - half) * (2 * C0 + 6 * C1 * x2)


def norm_rows(value):
    centre = value - jnp.mean(value, -1, keepdims=True)
    rstd = lax.rsqrt(jnp.mean(centre * centre, -1, keepdims=True) + EPS)
    return centre * rstd, rstd


def norm_rows_back(xhat, rstd, grad):
    return rstd * (
        grad
        - jnp.mean(grad, -1, keepdims=True)
        - xhat * jnp.mean(grad * xhat, -1, keepdims=True)
    )


def hot(index, rows):
    it = lax.broadcasted_iota(jnp.int32, (rows, index.shape[1]), 0)
    return jnp.where(it == index, 1.0, 0.0).astype(BF)


def side(refs):
    return jnp.concatenate(refs, 1)


def row_sum(value):
    return jnp.sum(value, 0, keepdims=True)


def vm(array):
    return (array, pl.BlockSpec(memory_space=pltpu.VMEM))


def out(shape, dtype):
    return (jax.ShapeDtypeStruct(shape, dtype), pl.BlockSpec(memory_space=pltpu.VMEM))


def dma(*shape):
    return pltpu.SemaphoreType.DMA(shape)


def remote(src, dst, send, recv, device):
    return pltpu.make_async_remote_copy(
        src_ref=src, dst_ref=dst, send_sem=send, recv_sem=recv, device_id=device, device_id_type=MESH
    )


def build(ids, parts, partners, steps, before, after):
    ins, outs, scr, bodies = {}, {}, {}, []
    for part in parts:
        ins.update(part.ins)
        outs.update(part.outs)
        scr.update(part.scr)
        if hasattr(part, "body"):
            bodies.append(part.body)
    names = list(ins) + list(outs) + list(scr)

    def kernel(*refs):
        e = SimpleNamespace(**dict(zip(names, refs, strict=True)))
        step = pl.program_id(0)

        def enter():
            barrier = pltpu.get_barrier_semaphore()
            devices = partners()
            for device in devices:
                pl.semaphore_signal(barrier, inc=1, device_id=device, device_id_type=MESH)
            pl.semaphore_wait(barrier, len(devices))

        def run(listed):
            for stage in listed:
                stage(e)

        for t in range(steps):
            if t == 0 or t in before:

                @pl.when(step == t)
                def _(t=t):
                    if t == 0:
                        enter()
                    run(before.get(t, ()))

        for body in bodies:
            body(e, step)
        for t in sorted(after):
            pl.when(step == t)(lambda t=t: run(after[t]))

    got = pl.pallas_call(
        kernel,
        grid=(steps,),
        out_shape=[shape for shape, _ in outs.values()],
        in_specs=[spec for _, spec in ins.values()],
        out_specs=[spec for _, spec in outs.values()],
        scratch_shapes=list(scr.values()),
        compiler_params=pltpu.CompilerParams(
            vmem_limit_bytes=VMEM_LIMIT, collective_id=next(ids), has_side_effects=True
        ),
    )(*[array for array, _ in ins.values()])
    return SimpleNamespace(**dict(zip(outs, got, strict=True)))


def place():
    return lax.axis_index("space"), lax.axis_index("nbr")


def wrap(value, count):
    return lax.rem(value + count, count)


def flip(value, bit):
    return value + (1 - 2 * (lax.rem(value // (1 << bit), 2))) * (1 << bit)


def across(axis, bit):
    s, n = place()
    return (s, flip(n, bit)) if axis == "nbr" else (flip(s, bit), n)


def near_cross(z):
    s, n = place()
    found = [(s, wrap(n + k, z.nn)) for k in range(1, z.nn)]
    sides = (1, -1) if z.ns > 2 else (1,)
    return found + [(wrap(s + d, z.ns), wrap(n + k, z.nn)) for d in sides for k in range(1, z.nn)]


def same_lane(z):
    s, n = place()
    return [(wrap(s + k, z.ns), n) for k in range(1, z.ns)]


def quarter(z):
    s, n = place()
    return pl.ds(pl.multiple_of(n * z.Q, 16), z.Q)


def far_copies(z, send, recv, fs, fr):
    s, n = place()
    found = []
    for k in range(1, z.ns):
        p = wrap(s + k, z.ns)
        found.append(
            remote(
                send.at[pl.ds(p * z.CAP, z.CAP)], recv.at[pl.ds(s * z.CAP, z.CAP)], fs.at[k], fr.at[k], (p, n)
            )
        )
    return found


def far_own(z, send, recv):
    s, n = place()
    here = pl.ds(pl.multiple_of(s * z.CAP, 8), z.CAP)
    recv[here] = send[here]


def setup_part(z, a):
    lines = (
        a.message_bias,
        a.edge_bias,
        a.edge_shift,
        a.third_gain,
        a.third_shift,
        a.message_shift,
        a.first_gain,
        a.first_shift,
        a.output_bias,
        a.second_gain,
        a.second_shift,
    )
    at = (0, 1, 2, 3, 4, 8, 9, 10, 11, 12, 13)

    def begin(e):
        e.vecs[...] = jnp.zeros_like(e.vecs)
        given = (e.va, e.vb, e.vc, e.vd, e.ve, e.vf, e.vg, e.vh, e.vi, e.vj, e.vk)
        for row, line in zip(at, given, strict=True):
            wide = line.shape[0]
            e.vecs[row : row + 1, 0:wide] = line[...].astype(F32).reshape(1, wide)
        hidden = e.vl[...].astype(F32).reshape(1, z.FF)
        for k in range(z.FF // z.DN):
            e.vecs[16 + k : 17 + k] = hidden[:, k * z.DN : (k + 1) * z.DN]
        p = lax.broadcasted_iota(jnp.int32, (z.CAP, z.FAR), 0)
        q = lax.broadcasted_iota(jnp.int32, (z.CAP, z.FAR), 1)
        spread = jnp.where(lax.rem(q, z.CAP) == p, 1.0, 0.0)
        b = lax.broadcasted_iota(jnp.int32, (z.ns, z.FAR), 0)
        c = lax.broadcasted_iota(jnp.int32, (z.ns, z.FAR), 1)
        for k in range(z.B):
            wide = jnp.dot(
                e.send_rows[k].astype(F32), spread, precision=lax.Precision.HIGHEST, preferred_element_type=F32
            )
            e.send[k] = (row_sum(jnp.where(c // z.CAP == b, wide, 0.0)) + 0.5).astype(jnp.int32)

    given = dict(zip("abcdefghijkl", lines + (a.hidden_bias,)))
    return SimpleNamespace(
        begin=begin,
        ins=dict({"v" + k: vm(v) for k, v in given.items()}, send_rows=vm(a.send_rows)),
        outs=dict(vecs=out((24, z.DN), F32), send=out((z.B, 1, z.FAR), jnp.int32)),
        scr={},
    )


def table_part(z, a):
    R, DN, FAR, TP, ns, B = z.R, z.DN, z.FAR, z.TP, z.ns, z.B
    half = R // 2

    def far(e, b):
        return far_copies(z, e.t_fsend.at[b], e.t_frecv.at[b], e.t_fs.at[b], e.t_fr.at[b])

    def near(e, b):
        s, n = place()
        h = pl.multiple_of(lax.rem(n, 2) * half, 16)
        src = e.nodes.at[b, pl.ds(h, half)]
        return [
            remote(
                src, e.t_tab.at[b, pl.ds(base + h, half)], e.t_ns.at[b, k], e.t_nr.at[b, k], (wrap(s + step, ns), n)
            )
            for k, (step, base) in enumerate(((1, 0), (-1, 2 * R)))
        ]

    def mate(e, b):
        s, n = place()
        h = pl.multiple_of(lax.rem(n, 2) * half, 16)
        found = []
        for k, base in enumerate((0, 2 * R)):
            rows = e.t_tab.at[b, pl.ds(base + h, half)]
            found.append(remote(rows, rows, e.t_ms.at[b, k], e.t_mr.at[b, k], (s, flip(n, 0))))
        return found

    def begin(b):
        def stage(e):
            for copy in near(e, b):
                copy.start()
            own = e.nodes[b]
            e.t_fsend[b] = dot_tn(hot(e.send[b], R), own)
            for copy in far(e, b):
                copy.start()
            e.t_tab[b, R : 2 * R] = own
            if TP > 3 * R + FAR:
                e.t_tab[b, 3 * R + FAR :] = jnp.zeros((TP - 3 * R - FAR, DN), BF)

        return stage

    def middle(b):
        def stage(e):
            for one, two in zip(near(e, b), mate(e, b), strict=True):
                one.wait_recv()
                two.start()

        return stage

    def finish(b):
        def stage(e):
            far_own(z, e.t_fsend.at[b], e.t_frecv.at[b])
            for copy in far(e, b):
                copy.wait()
            for copy in near(e, b):
                copy.wait_send()
            for copy in mate(e, b):
                copy.wait()
            e.t_tab[b, 3 * R : 3 * R + FAR] = e.t_frecv[b].astype(BF)
            e.tables[b] = e.t_tab[b]

        return stage

    return SimpleNamespace(
        begin=begin,
        middle=middle,
        finish=finish,
        ins=dict(nodes=vm(a.nodes)),
        outs=dict(tables=out((B, TP, DN), BF)),
        scr=dict(
            t_tab=pltpu.VMEM((B, TP, DN), BF),
            t_fsend=pltpu.VMEM((B, FAR, DN), F32),
            t_frecv=pltpu.VMEM((B, FAR, DN), F32),
            t_fs=dma(B, ns),
            t_fr=dma(B, ns),
            t_ns=dma(B, 2),
            t_nr=dma(B, 2),
            t_ms=dma(B, 2),
            t_mr=dma(B, 2),
        ),
    )


def message_part(z, a):
    R, DN, DE, TP, S, B = z.R, z.DN, z.DE, z.TP, z.S, z.B
    T = S // GROUP

    def body(e, step):
        sample, own = step // T, lax.rem(step, T)

        @pl.when(step == 0)
        def _():
            e.m_wst[...] = e.w_self[...].T
            e.m_wpt[...] = e.w_peer[...].T
            e.m_wet[...] = e.w_edge[...].T

        @pl.when(own == 0)
        def _():
            e.m_tabt[...] = dot_nt(e.m_wpt[...], e.t_tab[sample]).astype(BF)
            e.m_selft[...] = dot_nt(e.m_wst[...], e.nodes[sample]) + e.vecs[0:8].T[:, 0:1]
            e.m_acc[...] = jnp.zeros_like(e.m_acc)

        slots = [own * GROUP + g for g in range(GROUP)]
        line = pl.ds(sample, 1)
        value = dot(e.m_tabt[...], hot(side([e.nbr[s, line] for s in slots]), TP)) + dot(
            e.m_wet[...], side([e.m_edges[0, g] for g in range(GROUP)])
        )
        acc = e.m_acc[0:DN]
        count = e.m_acc[DN:]
        for g, s in enumerate(slots):
            live = e.live[s, line].astype(F32)
            act, slope = gelu_both(value[:, g * R : (g + 1) * R] + e.m_selft[...])
            e.slope[0, g] = slope.astype(BF)
            acc = acc + act * live
            count = count + live
        e.m_acc[0:DN] = acc
        e.m_acc[DN:] = count
        for b, ref in enumerate((e.part_a, e.part_b)):

            @pl.when(step == (b + 1) * T - 1)
            def _(ref=ref):
                ref[...] = e.m_acc[...].T.astype(BF)

    return SimpleNamespace(
        body=body,
        ins=dict(
            nodes=vm(a.nodes),
            m_edges=(a.edges_t, pl.BlockSpec((1, GROUP, DE, R), lambda i: (i // T, lax.rem(i, T), 0, 0))),
            nbr=vm(a.nbr),
            live=vm(a.live),
            w_self=vm(a.message_self),
            w_peer=vm(a.message_peer),
            w_edge=vm(a.message_edge),
        ),
        outs=dict(
            slope=(
                jax.ShapeDtypeStruct((B, S, DN, R), BF),
                pl.BlockSpec((1, GROUP, DN, R), lambda i: (i // T, lax.rem(i, T), 0, 0)),
            ),
            part_b=out((R, DN + LANES), BF),
        ),
        scr=dict(
            part_a=pltpu.VMEM((R, DN + LANES), BF),
            m_tabt=pltpu.VMEM((DN, TP), BF),
            m_selft=pltpu.VMEM((DN, R), F32),
            m_wst=pltpu.VMEM((DN, DN), BF),
            m_wpt=pltpu.VMEM((DN, DN), BF),
            m_wet=pltpu.VMEM((DN, DE), BF),
            m_acc=pltpu.VMEM((DN + LANES, R), F32),
        ),
    )


def forward_part(z, a, b, part):
    R, DN, DE, FF, Q, FAR, TP, ns, nn = z.R, z.DN, z.DE, z.FF, z.Q, z.FAR, z.TP, z.ns, z.nn
    W = DN + LANES

    def sums(e):
        s, n = place()
        found = []
        for k in range(1, nn):
            q = wrap(n + k, nn)
            rows = pl.ds(pl.multiple_of(q * Q, 16), Q)
            found.append(remote(part(e).at[rows], e.f_sum.at[k], e.f_ss.at[k], e.f_sr.at[k], (s, q)))
        return found

    def alls(e):
        s, n = place()
        rows = e.f_new.at[quarter(z)]
        return [
            remote(rows, rows, e.f_as.at[k], e.f_ar.at[k], (s, wrap(n + k, nn))) for k in range(1, nn)
        ]

    def near(e):
        s, n = place()
        found = []
        for i, (step, base) in enumerate(((1, 0), (-1, 2 * R))):
            rows = pl.ds(pl.multiple_of(base + n * Q, 16), Q)
            for k in range(nn):
                to = (wrap(s + step, ns), wrap(n + k, nn))
                found.append(remote(e.f_pe, e.f_tab.at[rows], e.f_ns.at[i, k], e.f_nr.at[i, k], to))
        return found

    def far(e):
        return far_copies(z, e.f_fsend, e.f_frecv, e.f_fs, e.f_fr)

    def begin(e):
        for copy in sums(e):
            copy.start()

    def compute(e):
        mine = quarter(z)
        for copy in sums(e):
            copy.wait()
        total = part(e)[mine].astype(F32)
        for k in range(1, nn):
            total = total + e.f_sum[k].astype(F32)
        count = total[:, DN : DN + 1]
        summed_act = total[:, :DN].astype(BF)
        summed = dot(summed_act, e.w_out[...]) + count * e.vecs[8:9]
        updated = e.nodes[b, mine].astype(F32) + summed / jnp.maximum(count, 1.0)
        xhat1, rstd1 = norm_rows(updated)
        hidden = xhat1 * e.vecs[9:10] + e.vecs[10:11]
        low = hidden.astype(BF)
        bias = side([e.vecs[16 + k : 17 + k] for k in range(FF // DN)])
        act, slope = gelu_both(dot(low, e.w_in[...]) + bias)
        act = act.astype(BF)
        xhat2, rstd2 = norm_rows(hidden + dot(act, e.w_ffn[...]) + e.vecs[11:12])
        fresh = (xhat2 * e.vecs[12:13] + e.vecs[13:14]).astype(BF)
        e.f_new[mine] = fresh
        e.f_pe[...] = dot_nt(fresh, e.ept[...]).astype(BF)
        for copy in alls(e):
            copy.start()
        for copy in near(e):
            copy.start()
        e.f_osum[...] = summed_act
        e.f_ocount[...] = total[:, DN:]
        e.f_ox1[...] = xhat1
        e.f_or1[...] = jnp.broadcast_to(rstd1, (Q, LANES))
        e.f_olow[...] = low
        e.f_oslope[...] = slope.astype(BF)
        e.f_oact[...] = act
        e.f_ox2[...] = xhat2
        e.f_or2[...] = jnp.broadcast_to(rstd2, (Q, LANES))
        e.f_oq[...] = fresh

    def spread(e):
        for copy in alls(e):
            copy.wait()
        own = dot_nt(e.f_new[...], e.ept[...]).astype(BF)
        e.f_tab[R : 2 * R] = own
        e.f_fsend[...] = dot_tn(hot(e.send[b], R), own)
        for copy in far(e):
            copy.start()
        e.f_onew[...] = e.f_new[...]
        if TP > 3 * R + FAR:
            e.f_tab[3 * R + FAR :] = jnp.zeros((TP - 3 * R - FAR, DE), BF)

    def finish(e):
        far_own(z, e.f_fsend, e.f_frecv)
        for copy in near(e):
            copy.wait()
        for copy in far(e):
            copy.wait()
        e.f_tab[3 * R : 3 * R + FAR] = e.f_frecv[...].astype(BF)
        e.f_otab[...] = e.f_tab[...]

    return SimpleNamespace(
        begin=begin,
        compute=compute,
        spread=spread,
        finish=finish,
        ins=dict(
            nodes=vm(a.nodes),
            w_out=vm(a.message_out),
            w_in=vm(a.hidden_in),
            w_ffn=vm(a.hidden_out),
            ept=vm(a.edge_peer_t),
        ),
        outs=dict(
            f_onew=out((R, DN), BF),
            f_otab=out((TP, DE), BF),
            f_osum=out((Q, DN), BF),
            f_ocount=out((Q, LANES), F32),
            f_ox1=out((Q, DN), F32),
            f_or1=out((Q, LANES), F32),
            f_olow=out((Q, DN), BF),
            f_oslope=out((Q, FF), BF),
            f_oact=out((Q, FF), BF),
            f_ox2=out((Q, DN), F32),
            f_or2=out((Q, LANES), F32),
            f_oq=out((Q, DN), BF),
        ),
        scr=dict(
            f_sum=pltpu.VMEM((nn, Q, W), BF),
            f_new=pltpu.VMEM((R, DN), BF),
            f_pe=pltpu.VMEM((Q, DE), BF),
            f_tab=pltpu.VMEM((TP, DE), BF),
            f_fsend=pltpu.VMEM((FAR, DE), F32),
            f_frecv=pltpu.VMEM((FAR, DE), F32),
            f_ss=dma(nn),
            f_sr=dma(nn),
            f_as=dma(nn),
            f_ar=dma(nn),
            f_ns=dma(2, nn),
            f_nr=dma(2, nn),
            f_fs=dma(ns),
            f_fr=dma(ns),
        ),
    )


def edge_part(z, a, first):
    R, DN, DE, TP, S, FAR, B = z.R, z.DN, z.DE, z.TP, z.S, z.FAR, z.B
    T = S // GROUP

    def body(e, step):
        sample, own = step // T, lax.rem(step, T)

        @pl.when(step == 0)
        def _():
            e.e_cols[...] = e.vecs[0:8].T[:DE]
            e.e_wnt[...] = e.e_wn[...].astype(F32).T.astype(BF)
            e.e_wot[...] = e.e_wo[...].astype(F32).T.astype(BF)
            for ref in (e.e_gacc, e.e_hacc, e.e_uacc, e.e_vacc, e.e_dwo, e.e_dwn):
                ref[...] = jnp.zeros_like(ref)

        for b, (table, fresh) in enumerate(((e.a_tab, e.a_new), (e.f_tab, e.f_new))):

            @pl.when(step == b * T)
            def _(table=table, fresh=fresh):
                e.e_tabt[...] = table[...].astype(F32).T.astype(BF)
                e.e_selft[...] = dot_nt(e.est[...], fresh[...]) + e.e_cols[:, 1:2]
                e.e_ptab[...] = jnp.zeros_like(e.e_ptab)
                e.e_sacc[...] = jnp.zeros_like(e.e_sacc)

        line = pl.ds(sample, 1)
        index = hot(side([e.nbr[own * GROUP + g, line] for g in range(GROUP)]), TP)
        edge = side([e.m_edges[0, g] for g in range(GROUP)])
        value = dot(e.e_tabt[...], index) + dot(e.e_wnt[...], edge)
        value = value + side([e.e_selft[...]] * GROUP)
        act, slope = gelu_both(value)
        act = act.astype(BF)
        shift_c, gain_c, bias_c = e.e_cols[:, 2:3], e.e_cols[:, 3:4], e.e_cols[:, 4:5]
        full = edge.astype(F32) + dot(e.e_wot[...], act) + shift_c
        full = full - jnp.mean(full, 0, keepdims=True)
        rstd = lax.rsqrt(jnp.mean(full * full, 0, keepdims=True) + EPS)
        xhat = full * rstd
        final = (xhat * gain_c + bias_c).astype(BF)
        cot = side([e.e_cot[0, g] for g in range(GROUP)]).astype(F32)
        scaled = cot * gain_c
        back = rstd * (
            scaled - jnp.mean(scaled, 0, keepdims=True) - xhat * jnp.mean(scaled * xhat, 0, keepdims=True)
        )
        low = back.astype(BF)
        e.e_dwo[...] += dot_nt(act, low)
        inner = (slope * dot(e.e_wo[...], low)).astype(BF)
        e.e_dwn[...] += dot_nt(edge, inner)
        part = (back + dot(e.e_wn[...], inner)).astype(BF)
        e.e_ptab[...] += dot_nt(inner, index)
        gain_g = cot * xhat
        low_f = low.astype(F32)
        inner_f = inner.astype(F32)
        s_acc, g_acc, h_acc, u_acc = e.e_sacc[...], e.e_gacc[...], e.e_hacc[...], e.e_uacc[...]
        for g in range(GROUP):
            cut = slice(g * R, (g + 1) * R)
            e.e_final[0, g] = final[:, cut]
            e.e_part[0, g] = part[:, cut]
            s_acc = s_acc + inner_f[:, cut]
            g_acc = g_acc + gain_g[:, cut]
            h_acc = h_acc + cot[:, cut]
            u_acc = u_acc + low_f[:, cut]
        e.e_sacc[...] = s_acc
        e.e_gacc[...] = g_acc
        e.e_hacc[...] = h_acc
        e.e_uacc[...] = u_acc
        ends = ((e.a_tgrad, e.a_fgrad, e.a_sgrad), (e.e_tgrad, e.e_fgrad, e.e_sgrad))
        for b, (tgrad, fgrad, sgrad) in enumerate(ends):

            @pl.when(step == (b + 1) * T - 1)
            def _(tgrad=tgrad, fgrad=fgrad, sgrad=sgrad):
                rows = e.e_ptab[...].T
                tgrad[...] = rows.astype(BF)
                fgrad[...] = rows[3 * R : 3 * R + FAR]
                turned = e.e_sacc[...].T
                sgrad[...] = turned.astype(BF)
                e.e_vacc[0:1] += row_sum(turned)

        @pl.when(step == B * T - 1)
        def _():
            for k, ref in enumerate((e.e_uacc, e.e_gacc, e.e_hacc)):
                e.e_vacc[k + 1 : k + 2] = row_sum(ref[...].T)
            e.e_vgrad[...] = e.e_vacc[...]

    stream = pl.BlockSpec((1, GROUP, DE, R), lambda i: (i // T, lax.rem(i, T), 0, 0))
    return SimpleNamespace(
        body=body,
        ins=dict(
            a_tab=vm(first.f_otab),
            a_new=vm(first.f_onew),
            m_edges=(a.edges_t, stream),
            e_cot=(a.cot_t, stream),
            nbr=vm(a.nbr),
            est=vm(a.edge_self_t),
            e_wn=vm(a.edge_own),
            e_wo=vm(a.edge_out),
        ),
        outs=dict(
            e_final=(jax.ShapeDtypeStruct((B, S, DE, R), BF), stream),
            e_part=(jax.ShapeDtypeStruct((B, S, DE, R), BF), stream),
            e_tgrad=out((TP, DE), BF),
            e_fgrad=out((FAR, DE), F32),
            e_sgrad=out((R, DE), BF),
            e_vgrad=out((8, DE), F32),
            e_dwo=out((DE, DE), F32),
            e_dwn=out((DE, DE), F32),
        ),
        scr=dict(
            a_tgrad=pltpu.VMEM((TP, DE), BF),
            a_fgrad=pltpu.VMEM((FAR, DE), F32),
            a_sgrad=pltpu.VMEM((R, DE), BF),
            e_tabt=pltpu.VMEM((DE, TP), BF),
            e_cols=pltpu.VMEM((DE, 8), F32),
            e_selft=pltpu.VMEM((DE, R), F32),
            e_wnt=pltpu.VMEM((DE, DE), BF),
            e_wot=pltpu.VMEM((DE, DE), BF),
            e_ptab=pltpu.VMEM((DE, TP), F32),
            e_sacc=pltpu.VMEM((DE, R), F32),
            e_gacc=pltpu.VMEM((DE, R), F32),
            e_hacc=pltpu.VMEM((DE, R), F32),
            e_uacc=pltpu.VMEM((DE, R), F32),
            e_vacc=pltpu.VMEM((8, DE), F32),
        ),
    )


def backward_part(z, a, b, node, grads):
    R, DN, DE, FF, Q, FAR, TP, ns, nn = z.R, z.DN, z.DE, z.FF, z.Q, z.FAR, z.TP, z.ns, z.nn
    W = DN + LANES

    def near(e):
        s, n = place()
        tgrad = grads(e)[0]
        return [
            remote(
                tgrad.at[pl.ds(base, R)], e.b_near.at[k], e.b_ns.at[k], e.b_nr.at[k], (wrap(s + step, ns), n)
            )
            for k, (step, base) in enumerate(((-1, 0), (1, 2 * R)))
        ]

    def far(e):
        return far_copies(z, grads(e)[1], e.b_frecv, e.b_fs, e.b_fr)

    def sums(e):
        s, n = place()
        found = []
        for k in range(1, nn):
            q = wrap(n + k, nn)
            rows = pl.ds(pl.multiple_of(q * Q, 16), Q)
            found.append(remote(e.b_pair.at[:, rows], e.b_sum.at[k], e.b_ss.at[k], e.b_sr.at[k], (s, q)))
        return found

    def alls(e):
        s, n = place()
        rows = e.b_all.at[quarter(z)]
        return [
            remote(rows, rows, e.b_as.at[k], e.b_ar.at[k], (s, wrap(n + k, nn))) for k in range(1, nn)
        ]

    def begin(e):
        for copy in near(e):
            copy.start()
        for copy in far(e):
            copy.start()

    def gather(e):
        tgrad, fgrad, sgrad = grads(e)
        far_own(z, fgrad, e.b_frecv)
        for copy in near(e):
            copy.wait()
        for copy in far(e):
            copy.wait()
        peer = (
            tgrad[R : 2 * R].astype(F32)
            + e.b_near[0].astype(F32)
            + e.b_near[1].astype(F32)
            + dot(hot(e.send[b], R), e.b_frecv[...].astype(BF))
        )
        e.b_pair[0] = peer.astype(BF)
        e.b_pair[1] = sgrad[...]
        for copy in sums(e):
            copy.start()

    def compute(e):
        mine = quarter(z)
        for copy in sums(e):
            copy.wait()
        peer = e.b_pair[0, mine].astype(F32)
        own = e.b_pair[1, mine].astype(F32)
        for k in range(1, nn):
            peer = peer + e.b_sum[k, 0].astype(F32)
            own = own + e.b_sum[k, 1].astype(F32)
        peer = peer.astype(BF)
        own = own.astype(BF)
        final = e.cot[b, mine].astype(F32) + dot(own, e.est[...]) + dot(peer, e.ept[...])
        xhat2 = e.b_x2[...]
        mid = norm_rows_back(xhat2, e.b_r2[:, 0:1], final * e.vecs[12:13])
        mid_low = mid.astype(BF)
        ffn = (e.b_slope[...].astype(F32) * dot_nt(mid_low, e.w_ffn[...])).astype(BF)
        hidden = mid + dot_nt(ffn, e.w_in[...])
        xhat1 = e.b_x1[...]
        grad = norm_rows_back(xhat1, e.b_r1[:, 0:1], hidden * e.vecs[9:10])
        count = e.b_count[:, 0:1]
        low = (grad / jnp.maximum(count, 1.0)).astype(BF)
        e.b_all[mine] = side([low, e.b_count[...].astype(BF)])
        for copy in alls(e):
            copy.start()
        e.b_omid[...] = mid_low
        e.b_offn[...] = ffn
        e.b_olow[...] = low
        e.b_opeer[...] = peer
        e.b_oself[...] = own
        wide = row_sum(ffn.astype(F32))
        e.b_ovec[...] = jnp.concatenate(
            [
                row_sum(low.astype(F32) * count),
                row_sum(hidden * xhat1),
                row_sum(hidden),
                row_sum(mid_low.astype(F32)),
                row_sum(final * xhat2),
                row_sum(final),
            ]
            + [wide[:, k * DN : (k + 1) * DN] for k in range(FF // DN)]
            + [jnp.zeros((6, DN), F32)],
            0,
        )

    def finish(e):
        for copy in alls(e):
            copy.wait()
        e.b_oall[...] = e.b_all[...]

    return SimpleNamespace(
        begin=begin,
        gather=gather,
        compute=compute,
        finish=finish,
        ins=dict(
            b_count=vm(node.f_ocount),
            b_x1=vm(node.f_ox1),
            b_r1=vm(node.f_or1),
            b_slope=vm(node.f_oslope),
            b_x2=vm(node.f_ox2),
            b_r2=vm(node.f_or2),
            cot=vm(a.node_cot),
            w_in=vm(a.hidden_in),
            w_ffn=vm(a.hidden_out),
            est=vm(a.edge_self_t),
            ept=vm(a.edge_peer_t),
        ),
        outs=dict(
            b_oall=out((R, W), BF),
            b_omid=out((Q, DN), BF),
            b_offn=out((Q, FF), BF),
            b_olow=out((Q, DN), BF),
            b_opeer=out((Q, DE), BF),
            b_oself=out((Q, DE), BF),
            b_ovec=out((16, DN), F32),
        ),
        scr=dict(
            b_near=pltpu.VMEM((2, R, DE), BF),
            b_frecv=pltpu.VMEM((FAR, DE), F32),
            b_pair=pltpu.VMEM((2, R, DE), BF),
            b_sum=pltpu.VMEM((nn, 2, Q, DE), BF),
            b_all=pltpu.VMEM((R, W), BF),
            b_ns=dma(2),
            b_nr=dma(2),
            b_fs=dma(ns),
            b_fr=dma(ns),
            b_ss=dma(nn),
            b_sr=dma(nn),
            b_as=dma(nn),
            b_ar=dma(nn),
        ),
    )


def last_part(z, a, spread, slope, part, tables):
    R, DN, DE, TP, S, FAR, B = z.R, z.DN, z.DE, z.TP, z.S, z.FAR, z.B
    T = S // GROUP

    def body(e, step):
        sample, own = step // T, lax.rem(step, T)
        for b, ref in enumerate((e.a_all, e.b_all)):

            @pl.when(step == b * T)
            def _(ref=ref, b=b):
                pltpu.make_async_copy(e.g_tables.at[b], e.g_tab, e.g_ts.at[b]).start()
                e.g_ht[...] = dot_nt(e.w_out[...], ref[:, 0:DN])
                e.g_ptab[...] = jnp.zeros_like(e.g_ptab)
                e.g_sacc[...] = jnp.zeros_like(e.g_sacc)
                if b == 0:
                    e.g_dwe[...] = jnp.zeros_like(e.g_dwe)
                    e.g_vec[...] = jnp.zeros_like(e.g_vec)

        line = pl.ds(sample, 1)
        slots = [own * GROUP + g for g in range(GROUP)]
        index = hot(side([e.nbr[s, line] for s in slots]), TP)
        edge = side([e.m_edges[0, g] for g in range(GROUP)])
        inner = []
        acc = e.g_sacc[...]
        for g, s in enumerate(slots):
            piece = (e.g_slope[0, g].astype(F32) * (e.g_ht[...] * e.live[s, line].astype(F32))).astype(BF)
            acc = acc + piece.astype(F32)
            inner.append(piece)
        e.g_sacc[...] = acc
        inner = side(inner)
        e.g_ptab[...] += dot_nt(inner, index)
        e.g_dwe[...] += dot_nt(edge, inner)
        back = dot(e.w_edge[...], inner)
        for g in range(GROUP):
            e.g_edge[0, g] = (back[:, g * R : (g + 1) * R] + e.g_part[0, g].astype(F32)).astype(BF)
        for b in range(B):

            @pl.when(step == (b + 1) * T - 1)
            def _(b=b):
                self_t = e.g_sacc[...].astype(BF)
                peer_t = e.g_ptab[...].astype(BF)
                pltpu.make_async_copy(e.g_tables.at[b], e.g_tab, e.g_ts.at[b]).wait()
                dself = dot(self_t, e.nodes[b])
                dpeer = dot(peer_t, e.g_tab[...])
                e.g_dself[...] = dself if b == 0 else e.g_dself[...] + dself
                e.g_dpeer[...] = dpeer if b == 0 else e.g_dpeer[...] + dpeer
                e.g_vec[0:1] += row_sum(e.g_sacc[...].T)
                e.o_rows[b] = dot(e.w_peer[...], peer_t).astype(BF)
                e.o_rows[b, :, R : 2 * R] = (
                    dot(e.w_peer[...], peer_t[:, R : 2 * R]) + dot(e.w_self[...], self_t)
                ).astype(BF)

    stream = pl.BlockSpec((1, GROUP, DE, R), lambda i: (i // T, lax.rem(i, T), 0, 0))
    return SimpleNamespace(
        body=body,
        ins=dict(
            a_all=vm(spread),
            g_slope=(slope, pl.BlockSpec((1, GROUP, DN, R), lambda i: (i // T, lax.rem(i, T), 0, 0))),
            g_part=(part, stream),
            g_tables=(tables, pl.BlockSpec(memory_space=pl.ANY)),
            nodes=vm(a.nodes),
            m_edges=(a.edges_t, stream),
            nbr=vm(a.nbr),
            live=vm(a.live),
            w_self=vm(a.message_self),
            w_peer=vm(a.message_peer),
            w_edge=vm(a.message_edge),
            w_out=vm(a.message_out),
        ),
        outs=dict(g_edge=(jax.ShapeDtypeStruct((B, S, DE, R), BF), stream)),
        scr=dict(
            g_tab=pltpu.VMEM((TP, DN), BF),
            g_ts=dma(B),
            g_ht=pltpu.VMEM((DN, R), F32),
            g_ptab=pltpu.VMEM((DN, TP), F32),
            g_sacc=pltpu.VMEM((DN, R), F32),
            g_dself=pltpu.VMEM((DN, DN), F32),
            g_dpeer=pltpu.VMEM((DN, DN), F32),
            g_dwe=pltpu.VMEM((DE, DN), F32),
            g_vec=pltpu.VMEM((8, DN), F32),
            o_rows=pltpu.VMEM((B, DN, TP), BF),
        ),
    )


def nodes_part(z, a, spreads):
    R, DN, FAR, TP, ns, nn, B = z.R, z.DN, z.FAR, z.TP, z.ns, z.nn, z.B
    L = DN // nn

    def sums(e, b):
        s, n = place()
        found = []
        for k in range(1, nn):
            q = wrap(n + k, nn)
            rows = pl.ds(pl.multiple_of(q * L, 16), L)
            found.append(remote(e.o_rows.at[b, rows], e.o_sum.at[b, k - 1], e.o_ss.at[b, k], e.o_sr.at[b, k], (s, q)))
        return found

    def near(e, b):
        s, n = place()
        return [
            remote(
                e.o_send.at[b, pl.ds(2 * k * R, R)],
                e.o_near.at[b, k],
                e.o_ns.at[b, k],
                e.o_nr.at[b, k],
                (wrap(s + step, ns), n),
            )
            for k, step in enumerate((-1, 1))
        ]

    def far(e, b):
        return far_copies(z, e.o_fsend.at[b], e.o_frecv.at[b], e.o_fs.at[b], e.o_fr.at[b])

    def begin(b):
        def stage(e):
            for copy in sums(e, b):
                copy.start()

        return stage

    def middle(b):
        def stage(e):
            s, n = place()
            for copy in sums(e, b):
                copy.wait()
            total = e.o_rows[b, pl.ds(pl.multiple_of(n * L, 16), L)].astype(F32)
            for k in range(1, nn):
                total = total + e.o_sum[b, k - 1].astype(F32)
            turned = total.T
            e.o_send[b] = turned.astype(BF)
            e.o_fsend[b] = turned[3 * R : 3 * R + FAR]
            for copy in near(e, b):
                copy.start()
            for copy in far(e, b):
                copy.start()
            column = pl.ds(pl.multiple_of(n * L, L), L)
            spread = spreads(e)[b]
            count = spread[:, DN : DN + 1].astype(F32)
            e.o_grad[b] = turned[R : 2 * R] + spread[:, column].astype(F32) * jnp.maximum(count, 1.0)

        return stage

    def finish(b):
        def stage(e):
            far_own(z, e.o_fsend.at[b], e.o_frecv.at[b])
            for copy in near(e, b):
                copy.wait()
            for copy in far(e, b):
                copy.wait()
            e.o_grad[b] += (
                e.o_near[b, 0].astype(F32)
                + e.o_near[b, 1].astype(F32)
                + dot(hot(e.send[b], R), e.o_frecv[b].astype(BF))
            )

        return stage

    return SimpleNamespace(
        begin=begin,
        middle=middle,
        finish=finish,
        ins={},
        outs=dict(o_grad=out((B, R, L), F32)),
        scr=dict(
            o_sum=pltpu.VMEM((B, nn - 1, L, TP), BF),
            o_send=pltpu.VMEM((B, TP, L), BF),
            o_near=pltpu.VMEM((B, 2, R, L), BF),
            o_fsend=pltpu.VMEM((B, FAR, L), F32),
            o_frecv=pltpu.VMEM((B, FAR, L), F32),
            o_ss=dma(B, nn),
            o_sr=dma(B, nn),
            o_ns=dma(B, 2),
            o_nr=dma(B, 2),
            o_fs=dma(B, ns),
            o_fr=dma(B, ns),
        ),
    )


def cut(z, total, start):
    unit = 16 << SPLITS
    units = max(3, -(-total // unit))
    sizes = [units // 3 + (1 if k < units % 3 else 0) for k in range(3)]
    starts = [start + sum(sizes[:k]) * unit for k in range(3)]
    return start + units * unit, [(at, size * unit) for at, size in zip(starts, sizes)]


def bit_orders(z):
    nbr = [("nbr", k) for k in range(z.nn.bit_length() - 1)]
    space = [("space", k) for k in range(z.ns.bit_length() - 1)]
    first, ring, rest = nbr[:1], [nbr[1], space[0], space[1]], nbr[2:] + space[2:]
    return [first + ring[k:] + ring[:k] + rest[: SPLITS - 4] for k in range(3)], rest[SPLITS - 4 :]


def pack_rows(z):
    DN, DE, FF = z.DN, z.DE, z.FF
    early = dict(wi=FF, wf=FF, wo=DN, es=DE, ep=DE)
    late = dict(ws=DN, wp=DN, we=DE, own=DE, vec=32)
    at, row = SimpleNamespace(), 0
    for group in (early, late):
        first = row
        for name, size in group.items():
            setattr(at, name, row)
            row += size
        used = row
        row, parts = cut(z, used - first, first)
        if group is early:
            at.early, at.early_end = parts, used
        else:
            at.late, at.late_end = parts, used
    at.rows = row
    at.middle = at.late[0][0]
    return at


def sum_part(z, a, at, early):
    DN, DE, FF, B = z.DN, z.DE, z.FF, z.B
    orders, whole = bit_orders(z)
    phases = len(orders[0])
    most = max(size for _, size in at.early + at.late) >> phases
    parts = at.early + at.late
    groups = (range(3), range(3, 6))

    def bit_value(axis, bit):
        s, n = place()
        return lax.rem((n if axis == "nbr" else s) // (1 << bit), 2)

    def segment(part, depth):
        start, size = parts[part]
        for axis, bit in orders[part % 3][:depth]:
            size //= 2
            start = start + bit_value(axis, bit) * size
        return start, size

    def down(e, part, depth):
        axis, bit = orders[part % 3][depth]
        start, size = segment(part, depth)
        size //= 2
        give = pl.multiple_of(start + (1 - bit_value(axis, bit)) * size, 16)
        base = parts[part][0] + parts[part][1] - 2 * size
        copy = remote(
            e.s_buf.at[pl.ds(give, size)],
            e.s_recv.at[pl.ds(base, size)],
            e.s_ds.at[part, depth],
            e.s_dr.at[part, depth],
            across(axis, bit),
        )
        return copy, size, base

    def up(e, part, depth):
        start, size = segment(part, depth + 1)
        rows = pl.ds(pl.multiple_of(start, 16), size)
        src = e.s_buf if depth == phases - 1 else e.s_out
        return remote(
            src.at[rows],
            e.s_out.at[rows],
            e.s_us.at[part, depth],
            e.s_ur.at[part, depth],
            across(*orders[part % 3][depth]),
        )

    def keep_own(e, part):
        start, size = segment(part, phases)
        rows = pl.ds(pl.multiple_of(start, 16), size)
        return pltpu.make_async_copy(e.s_buf.at[rows], e.s_out.at[rows], e.s_os.at[part])

    def begin(group):
        def stage(e):
            for part in groups[group]:
                down(e, part, 0)[0].start()

        return stage

    def fold(group, depth):
        def stage(e):
            for part in groups[group]:
                copy, size, base = down(e, part, depth)
                copy.wait()
                start, _ = segment(part, depth + 1)
                keep = pl.ds(pl.multiple_of(start, 16), size)
                value = (e.s_buf[keep].astype(F32) + e.s_recv[pl.ds(base, size)].astype(F32)).astype(BF)
                if depth + 1 < phases:
                    e.s_buf[keep] = value
                    down(e, part, depth + 1)[0].start()
                    continue
                for k, (axis, bit) in enumerate(whole):
                    e.s_buf[keep] = value
                    copy = remote(
                        e.s_buf.at[keep],
                        e.s_more.at[part, k, pl.ds(0, size)],
                        e.s_ms.at[part, k],
                        e.s_mr.at[part, k],
                        across(axis, bit),
                    )
                    copy.start()
                    copy.wait()
                    value = (value.astype(F32) + e.s_more[part, k, 0:size].astype(F32)).astype(BF)
                e.s_buf[keep] = value
                keep_own(e, part).start()
                up(e, part, depth).start()

        return stage

    def spread(group, depth):
        def stage(e):
            for part in groups[group]:
                up(e, part, depth).wait()
                if depth == phases - 1:
                    keep_own(e, part).wait()
                if depth:
                    up(e, part, depth - 1).start()

        return stage

    def put(e, row, value):
        e.s_buf[row : row + value.shape[0], : value.shape[1]] = value.astype(BF)

    def clear(e, first, last):
        if last > first:
            e.s_buf[first:last] = jnp.zeros((last - first, DN), BF)

    def pack_early(e):
        def two(one, other):
            return jnp.concatenate([one[...], other[...]], 0)

        low, ffn = two(e.p_low0, e.p_low1), two(e.p_ffn0, e.b_offn)
        act, mid = two(e.p_act0, e.p_act1), two(e.p_mid0, e.b_omid)
        for k in range(FF // DN):
            put(e, at.wi + k * DN, dot_tn(low, ffn[:, k * DN : (k + 1) * DN]))
        for k in range(FF // DN):
            put(e, at.wf + k * DN, dot_tn(act[:, k * DN : (k + 1) * DN], mid))
        put(e, at.wo, dot_tn(two(e.p_sum0, e.p_sum1), two(e.p_grad0, e.b_olow)))
        fresh = two(e.p_new0, e.p_new1)
        put(e, at.es, dot_tn(two(e.p_self0, e.b_oself), fresh))
        put(e, at.ep, dot_tn(two(e.p_peer0, e.b_opeer), fresh))
        clear(e, at.early_end, at.middle)

    def pack_late(e):
        put(e, at.ws, e.g_dself[...].T)
        put(e, at.wp, e.g_dpeer[...].T)
        put(e, at.we, e.g_dwe[...])
        gap = jnp.zeros((DE, 256 - DE), F32)
        put(e, at.own, side([e.p_dwn[...], gap, e.p_dwo[...], gap]))
        narrow = side([e.p_vec[...], jnp.zeros((8, DN - DE), F32)])
        put(e, at.vec, jnp.concatenate([e.p_vec0[...] + e.b_ovec[...], narrow, e.g_vec[...]], 0))
        clear(e, at.late_end, at.rows)

    f0, f1, b0, ee = early
    return SimpleNamespace(
        begin=begin,
        fold=fold,
        spread=spread,
        pack_early=pack_early,
        pack_late=pack_late,
        phases=phases,
        ins=dict(
            p_low0=vm(f0.f_olow),
            p_low1=vm(f1.f_olow),
            p_act0=vm(f0.f_oact),
            p_act1=vm(f1.f_oact),
            p_sum0=vm(f0.f_osum),
            p_sum1=vm(f1.f_osum),
            p_new0=vm(f0.f_oq),
            p_new1=vm(f1.f_oq),
            p_ffn0=vm(b0.b_offn),
            p_mid0=vm(b0.b_omid),
            p_grad0=vm(b0.b_olow),
            p_self0=vm(b0.b_oself),
            p_peer0=vm(b0.b_opeer),
            p_vec0=vm(b0.b_ovec),
            p_vec=vm(ee.e_vgrad),
            p_dwo=vm(ee.e_dwo),
            p_dwn=vm(ee.e_dwn),
        ),
        outs=dict(s_out=(jax.ShapeDtypeStruct((at.rows, DN), BF), pl.BlockSpec(memory_space=pl.ANY))),
        scr=dict(
            s_buf=pltpu.VMEM((at.rows, DN), BF),
            s_recv=pltpu.VMEM((at.rows, DN), BF),
            s_os=dma(6),
            s_more=pltpu.VMEM((6, len(whole), most, DN) if whole else (16, DN), BF),
            s_ms=dma(6, max(1, len(whole))),
            s_mr=dma(6, max(1, len(whole))),
            s_ds=dma(6, phases),
            s_dr=dma(6, phases),
            s_us=dma(6, phases),
            s_ur=dma(6, phases),
        ),
    )


def unpack_kernel(z, packed, at):
    DN, DE, FF = z.DN, z.DE, z.FF

    def kernel(p, ws, wp, we, wo, wi, wf, es, ep, own, eo, *vectors):
        def get(row, size):
            return p[row : row + size].astype(F32)

        ws[...] = get(at.ws, DN)
        wp[...] = get(at.wp, DN)
        we[...] = get(at.we, DE)
        wo[...] = get(at.wo, DN)
        for k in range(FF // DN):
            wi[:, k * DN : (k + 1) * DN] = get(at.wi + k * DN, DN)
        wf[...] = get(at.wf, FF)
        es[...] = get(at.es, DE)
        ep[...] = get(at.ep, DE)
        pair = get(at.own, DE)
        own[...] = pair[:, :DE]
        eo[...] = pair[:, 256 : 256 + DE]
        vec = get(at.vec, 32)
        hidden = side([vec[6 + k : 7 + k] for k in range(FF // DN)])
        vectors[0][...] = hidden.reshape(FF)
        for ref, row in zip(vectors[1:], (24, 0, 1, 2, 3, 4, 5, 16, 17, 18, 19), strict=True):
            wide = ref.shape[0]
            ref[...] = vec[row : row + 1, :wide].reshape(wide)

    shapes = [(DN, DN), (DN, DN), (DE, DN), (DN, DN), (DN, FF), (FF, DN), (DE, DN), (DE, DN), (DE, DE), (DE, DE)]
    shapes += [(FF,)] + [(DN,)] * 7 + [(DE,)] * 4
    return pl.pallas_call(
        kernel,
        out_shape=[jax.ShapeDtypeStruct(shape, F32) for shape in shapes],
        in_specs=[pl.BlockSpec(memory_space=pltpu.VMEM)],
        out_specs=[pl.BlockSpec(memory_space=pltpu.VMEM)] * len(shapes),
        compiler_params=pltpu.CompilerParams(vmem_limit_bytes=VMEM_LIMIT),
    )(packed)


def local(
    nodes,
    edges,
    neighbors,
    slot_live,
    send_rows,
    message_self,
    message_peer,
    message_edge,
    message_bias,
    message_out,
    message_shift,
    first_gain,
    first_shift,
    hidden_in,
    hidden_bias,
    hidden_out,
    output_bias,
    second_gain,
    second_shift,
    edge_self,
    edge_peer,
    edge_own,
    edge_bias,
    edge_out,
    edge_shift,
    third_gain,
    third_shift,
    node_cot,
    edge_cot,
):
    a = SimpleNamespace(**locals())
    B, R, DN = nodes.shape
    S, DE = edges.shape[2:]
    ns, nn = lax.axis_size("space"), lax.axis_size("nbr")
    CAP = send_rows.shape[2]
    FAR = ns * CAP
    TP = -(-(3 * R + FAR) // LANES) * LANES
    z = SimpleNamespace(
        B=B, R=R, DN=DN, S=S, DE=DE, ns=ns, nn=nn, CAP=CAP, FAR=FAR, TP=TP, FF=hidden_in.shape[1], Q=R // nn
    )
    ids = itertools.count(1)
    a.edges_t = edges.transpose(0, 2, 3, 1)
    a.cot_t = edge_cot.transpose(0, 2, 3, 1)
    a.nbr = neighbors.transpose(2, 0, 1)
    a.live = slot_live.transpose(2, 0, 1)
    a.edge_self_t, a.edge_peer_t = edge_self.T, edge_peer.T
    T = S // GROUP

    def plain(part):
        return SimpleNamespace(ins=part, outs={}, scr={})

    small, table, message = setup_part(z, a), table_part(z, a), message_part(z, a)
    node0 = forward_part(z, a, 0, lambda e: e.part_a)
    f0 = build(
        ids,
        [small, table, message, node0],
        lambda: near_cross(z) + same_lane(z),
        2 * T,
        {0: [small.begin, table.begin(0), table.middle(0), table.begin(1), table.finish(0)], T: [node0.begin]},
        {
            1: [table.middle(1)],
            3: [table.finish(1)],
            T + 1: [node0.compute],
            T + 3: [node0.spread],
            2 * T - 1: [node0.finish],
        },
    )
    shared = plain(dict(vecs=vm(f0.vecs), send=vm(f0.send)))

    edge = edge_part(z, a, f0)
    node1 = forward_part(z, a, 1, lambda e: e.part_b)
    back0 = backward_part(z, a, 0, f0, lambda e: (e.a_tgrad, e.a_fgrad, e.a_sgrad))
    f1 = build(
        ids,
        [shared, plain(dict(part_b=vm(f0.part_b))), edge, node1, back0],
        lambda: near_cross(z) + same_lane(z),
        2 * T,
        {0: [node1.begin], T: [back0.begin]},
        {
            1: [node1.compute],
            3: [node1.spread],
            T - 1: [node1.finish],
            T + 1: [back0.gather],
            T + 2: [back0.compute],
            2 * T - 1: [back0.finish],
        },
    )

    at = pack_rows(z)
    last = last_part(z, a, f1.b_oall, f0.slope, f1.e_part, f0.tables)
    back1 = backward_part(z, a, 1, f1, lambda e: (e.e_tgrad, e.e_fgrad, e.e_sgrad))
    outer = nodes_part(z, a, lambda e: (e.a_all, e.b_all))
    total = sum_part(z, a, at, (f0, f1, f1, f1))
    for name, (shape, spec) in back1.outs.items():
        back1.scr[name] = pltpu.VMEM(shape.shape, shape.dtype)
    back1.outs = {}
    D = total.phases
    tail = [outer.begin(1), total.pack_late, total.begin(1), total.fold(0, D - 1)]
    tail += [total.fold(1, 0), outer.middle(1)]
    for d in reversed(range(D)):
        tail.append(total.spread(0, d))
        if D - d < D:
            tail.append(total.fold(1, D - d))
        if d == D - 3:
            tail.append(outer.finish(1))
    tail += [total.spread(1, d) for d in reversed(range(D))]
    after = {
        1: [back1.gather],
        2: [back1.compute, total.pack_early, total.begin(0)],
        3: [total.fold(0, 0)],
        T - 1: [back1.finish],
        T + 1: [total.fold(0, 1)],
        T + 2: [outer.middle(0), total.fold(0, 2)],
        2 * T - 1: [outer.finish(0)] + [total.fold(0, d) for d in range(3, D - 1)] + tail,
    }
    grads = dict(e_tgrad=vm(f1.e_tgrad), e_fgrad=vm(f1.e_fgrad), e_sgrad=vm(f1.e_sgrad))
    f2 = build(
        ids,
        [shared, plain(grads), last, back1, outer, total],
        lambda: [(lax.axis_index("space"), wrap(lax.axis_index("nbr") + k, nn)) for k in range(1, nn)] + same_lane(z),
        2 * T,
        {0: [back1.begin], T: [outer.begin(0)]},
        after,
    )
    ws, wp, we, wo, wi, wf, es, ep, own, eo, *vectors = unpack_kernel(z, f2.s_out, at)
    hidden, mb, ms, fg, fs, ob, sg, ss, eb, esh, tg, ts = vectors
    return (
        jnp.stack([f0.f_onew, f1.f_onew]),
        f1.e_final.transpose(0, 3, 1, 2),
        f2.o_grad,
        f2.g_edge.transpose(0, 3, 1, 2),
        ws,
        wp,
        we,
        mb,
        wo,
        ms,
        fg,
        fs,
        wi,
        hidden,
        wf,
        ob,
        sg,
        ss,
        es.T,
        ep.T,
        own,
        eb,
        eo,
        esh,
        tg,
        ts,
    )


def solution(mesh):
    tall = P(None, "space", None)
    slots = P(None, "space", "nbr", None)
    marks = P(None, "space", "nbr")
    return jax.shard_map(
        local,
        mesh=mesh,
        in_specs=(tall, slots, marks, marks, tall) + (P(),) * 22 + (tall, slots),
        out_specs=(tall, slots, marks, slots) + (P(),) * 22,
        check_vma=False,
    )
```

time: 1330 us -> 286 us (0.22); the launches traced: 1310 us -> 286 us
  local copies, waits for them, and re-layouts: 452 us -> 7.81 us
  Pallas kernels: 0 us -> 276 us
  other arithmetic: 271 us -> 1.95 us
  matrix products: 236 us -> 0 us
  waiting for transfers between devices: 191 us -> 0 us
  starting transfers between devices: 98.7 us -> 0 us
  blocking collectives: 47.1 us -> 0 us
  between operations: 16.5 us -> 0.75 us
    pallas_call x0 -> x4, Pallas kernels: none -> 276 us  [the longest x3 268 us: build(): pl.pallas_call(kernel, grid=(steps,), out_shape=[shape for shape, _ in ou...]
    dot_general x60 -> x0, matrix products: 236 us -> none  [the longest x20 91.5 us: back_product(): lax.dot_general(left, right, (((1,), (1,)), ((), ())), preferred_element_...]
    psum x3 -> x0, waiting for transfers between devices: 188 us -> none  [the longest x1 148 us: local(): lax.psum((running[0], running[1], running[2], running[3], running[4], run...]
    scatter-add x8 -> x0, other arithmetic: 150 us -> none  [the longest x2 78.9 us: local(): node_table_grad = jax.ops.segment_sum(inner_wide, index_flat, table_rows)]
    gather x10 -> x0, local copies, waits for them, and re-layouts: 85.7 us -> none  [the longest x4 43.4 us: local(): edge_gathered = edge_table[index_flat].astype(WIDE)]
    convert_element_type x22 -> x0, local copies, waits for them, and re-layouts: 74.4 us -> none  [the longest x6 40 us: local(): edge_cot[sample].reshape(edge_total, edge_width).astype(WIDE)]
    add x10 -> x0, local copies, waits for them, and re-layouts: 71.9 us -> none  [the longest x4 37.4 us: local(): (gathered + product(edge_flat, message_edge) + message_bias.astype(WIDE))...]
    reduce_sum x26 -> x0, other arithmetic: 69.9 us -> none  [the longest x2 15.4 us: local(): jnp.sum(inner_wide.reshape(block_rows, slot_count, node_width), 1)]
  transfers between devices with their start and end apart: 29 -> 0, of which waited for: 3 -> 0; matrix products, arithmetic and copies ran while one was open for 33% -> 0% of each run, Pallas kernels for 0% -> 0%
where the time goes in v1:
time: 286 us
  Pallas kernels  276 us (97%)
  local copies, waits for them, and re-layouts  7.81 us (3%)
    pallas_call x3, Pallas kernels, build(): pl.pallas_call(kernel, grid=(steps,), out_shape=[shape for shape, _ in ou...  268 us
    pallas_call x1, Pallas kernels, unpack_kernel(): pl.pallas_call(kernel, out_shape=[jax.ShapeDtypeStruct(shape, F32) for sh...  7.84 us
    unnamed x11, local copies, waits for them, and re-layouts  7.81 us

profile of v1, /device:TPU:0, one launch (start us, length us, event | category | flops | bytes accessed | tf_op | source)
XLA Modules:
  0.0 286.3 jit_solution(5150420458274942853)
XLA Ops:
  0.7 67.1 %shard_map.476 = (f32[24,512]{1,0:T(8,128)}, s32[2,1,64]{2,1,0:T(1,128)}, bf16[2,1280,512]{2,1,0:T(8,128)(2,1)}, bf16[2,15,512,384]{3,2,1,0:T(8,128)(2,1)}, bf16...) custom-call(bf16[512]{0:T(512)(128)(2,1)} %refs_0_.1, ...), custom_call_target="tpu_custom_call" | custom-call | tf_op jit(solution)/shard_map/pallas_call | solution.py:126
  67.8 0.0 copy-start
  67.8 62.3 %shard_map.477 = (bf16[2,15,192,384]{3,2,1,0:T(8,128)(2,1)}, bf16[2,15,192,384]{3,2,1,0:T(8,128)(2,1)}, bf16[1280,192]{1,0:T(8,128)(2,1)}, f32[64,192]{1,0:T(8,1...) custom-call(f32[24,512]{1,0:T(8,128)} %get-tuple-element.95.refs_0_,, ...), custom_call_target="tpu_custom_call" | custom-call | tf_op jit(solution)/shard_map/pallas_call | solution.py:126
  130.0 0.0 copy-done
  130.0 1.9 pad_maximum_fusion
  132.0 138.6 %shard_map.478 = (bf16[2,15,192,384]{3,2,1,0:T(8,128)(2,1)}, f32[2,384,128]{2,1,0:T(8,128)}, bf16[6656,512]{1,0:T(8,128)(2,1)}) custom-call(f32[24,512]{1,0:T(8,128)} %get-tuple-element.95.refs_0_, s32[2,1,64]{2,1,0:T(1,128)} %get-tuple-element.96.refs_1_, bf16[1280,192]{1,0:T(8,128)(2,1)} %get-tuple-element.107.refs_2_, ...), custom_call_target="tpu_custom_call" | custom-call | tf_op jit(solution)/shard_map/pallas_call | solution.py:126
  270.6 0.0 slice-start
  270.7 7.8 %shard_map.479 = (f32[512,512]{1,0:T(8,128)}, f32[512,512]{1,0:T(8,128)}, f32[192,512]{1,0:T(8,128)}, f32[512,512]{1,0:T(8,128)}, f32[512,2048]{1,0:T(8,128)}, /...) custom-call(bf16[6656,512]{1,0:T(8,128)(2,1)} %get-tuple-element.139.p), custom_call_target="tpu_custom_call" | custom-call | tf_op jit(solution)/shard_map/pallas_call | solution.py:1224
  278.5 0.0 copy-start.1
  278.5 0.0 slice-start.1
  278.5 5.0 %copy.58 = bf16[2,384,15,192]{1,3,2,0:T(8,128)(2,1)} copy(bf16[2,384,15,192]{1,3,2,0:T(8,128)(2,1)} %bitcast.16) | data formatting | bytes 8847360
  283.5 0.0 copy-done.1
  283.5 0.7 copy.59
  284.2 0.0 slice-done
  284.2 0.0 slice-done.1
  284.2 2.1 copy.60
  (1 shorter events, 0.0 us)
Async XLA Ops:
  67.8 62.3 %copy-start = (bf16[384,512]{1,0:T(8,128)(2,1)S(1)}, bf16[384,512]{1,0:T(8,128)(2,1)}, u32[]{:S(2)}) copy-start(bf16[384,512]{1,0:T(8,128)(2,1)} %get-tuple-element.94.refs_4_) | copy-start | bytes 1179652
  270.6 13.6 %slice-start = ((s8[4423680]{0:T(1024)(128)(4,1)}), s8[229376]{0:T(1024)(128)(4,1)S(1)}, s32[]{:S(2)}) async-start(s8[4423680]{0:T(1024)(128)(4,1)} %bitcast.17), calls=%async_computation | async-start | bytes 458752
  278.5 5.0 %copy-start.1 = (f32[2,384,128]{2,1,0:T(8,128)S(1)}, f32[2,384,128]{2,1,0:T(8,128)}, u32[]{:S(2)}) copy-start(f32[2,384,128]{2,1,0:T(8,128)} %get-tuple-element.190) | copy-start | bytes 1179652
  278.5 5.7 %slice-start.1 = ((s8[4423680]{0:T(1024)(128)(4,1)}), s8[4194304]{0:T(1024)(128)(4,1)S(1)}, s32[]{:S(2)}) async-start(s8[4423680]{0:T(1024)(128)(4,1)} %bitcast.17), calls=%async_computation.1 | async-start | bytes 8388608

commit v2 on v1

--- a/solution.py
+++ b/solution.py
@@ -18,6 +18,7 @@
 GROUP = 3
 LANES = 128
 SPLITS = 5
+ROUNDS = 2
 
 
 def dot(left, right):
@@ -33,10 +34,12 @@
 
 
 def gelu_both(x):
+    one = jnp.ones((), x.dtype)
+    a, b = one * C0, one * C1
     x2 = x * x
-    half = 0.5 * jnp.tanh(x * (C0 + C1 * x2)) + 0.5
+    half = one * 0.5 * jnp.tanh(x * (a + b * x2)) + one * 0.5
     act = x * half
-    return act, half + act * (1.0 - half) * (2 * C0 + 6 * C1 * x2)
+    return act, half + act * (one - half) * (one * (2 * C0) + one * (6 * C1) * x2)
 
 
 def norm_rows(value):
@@ -84,7 +87,7 @@
     )
 
 
-def build(ids, parts, partners, steps, before, after):
+def build(ids, parts, partners, steps, before, after, later=()):
     ins, outs, scr, bodies = {}, {}, {}, []
     for part in parts:
         ins.update(part.ins)
@@ -92,11 +95,22 @@
         scr.update(part.scr)
         if hasattr(part, "body"):
             bodies.append(part.body)
+    for name in later:
+        array, _ = ins.pop(name)
+        ins["h_" + name] = (array, pl.BlockSpec(memory_space=pl.ANY))
+        scr[name] = pltpu.VMEM(array.shape, array.dtype)
+    scr["l_sem"] = dma(max(1, len(later)))
     names = list(ins) + list(outs) + list(scr)
 
     def kernel(*refs):
         e = SimpleNamespace(**dict(zip(names, refs, strict=True)))
         step = pl.program_id(0)
+
+        def bring():
+            return [
+                pltpu.make_async_copy(getattr(e, "h_" + name), getattr(e, name), e.l_sem.at[k])
+                for k, name in enumerate(later)
+            ]
 
         def enter():
             barrier = pltpu.get_barrier_semaphore()
@@ -107,7 +121,11 @@
 
         def run(listed):
             for stage in listed:
-                stage(e)
+                if stage is ready:
+                    for copy in bring():
+                        copy.wait()
+                else:
+                    stage(e)
 
         for t in range(steps):
             if t == 0 or t in before:
@@ -115,6 +133,8 @@
                 @pl.when(step == t)
                 def _(t=t):
                     if t == 0:
+                        for copy in bring():
+                            copy.start()
                         enter()
                     run(before.get(t, ()))
 
@@ -135,6 +155,10 @@
         ),
     )(*[array for array, _ in ins.values()])
     return SimpleNamespace(**dict(zip(outs, got, strict=True)))
+
+
+def ready(e):
+    raise NotImplementedError
 
 
 def place():
@@ -574,7 +598,7 @@
         inner = (slope * dot(e.e_wo[...], low)).astype(BF)
         e.e_dwn[...] += dot_nt(edge, inner)
         part = (back + dot(e.e_wn[...], inner)).astype(BF)
-        e.e_ptab[...] += dot_nt(inner, index)
+        e.e_ptab[...] += dot_nt(index, inner)
         gain_g = cot * xhat
         low_f = low.astype(F32)
         inner_f = inner.astype(F32)
@@ -596,7 +620,7 @@
 
             @pl.when(step == (b + 1) * T - 1)
             def _(tgrad=tgrad, fgrad=fgrad, sgrad=sgrad):
-                rows = e.e_ptab[...].T
+                rows = e.e_ptab[...]
                 tgrad[...] = rows.astype(BF)
                 fgrad[...] = rows[3 * R : 3 * R + FAR]
                 turned = e.e_sacc[...].T
@@ -641,7 +665,7 @@
             e_selft=pltpu.VMEM((DE, R), F32),
             e_wnt=pltpu.VMEM((DE, DE), BF),
             e_wot=pltpu.VMEM((DE, DE), BF),
-            e_ptab=pltpu.VMEM((DE, TP), F32),
+            e_ptab=pltpu.VMEM((TP, DE), F32),
             e_sacc=pltpu.VMEM((DE, R), F32),
             e_gacc=pltpu.VMEM((DE, R), F32),
             e_hacc=pltpu.VMEM((DE, R), F32),
@@ -891,13 +915,28 @@
     R, DN, FAR, TP, ns, nn, B = z.R, z.DN, z.FAR, z.TP, z.ns, z.nn, z.B
     L = DN // nn
 
+    pairs = nn // 2
+
+    def mates(e, b):
+        s, n = place()
+        other = flip(n, 0)
+        found = []
+        for k in range(pairs):
+            q = lax.rem(other, 2) + 2 * k
+            rows = pl.ds(pl.multiple_of(q * L, 16), L)
+            found.append(
+                remote(e.o_rows.at[b, rows], e.o_half.at[b, k], e.o_hs.at[b, k], e.o_hr.at[b, k], (s, other))
+            )
+        return found
+
     def sums(e, b):
         s, n = place()
         found = []
-        for k in range(1, nn):
-            q = wrap(n + k, nn)
-            rows = pl.ds(pl.multiple_of(q * L, 16), L)
-            found.append(remote(e.o_rows.at[b, rows], e.o_sum.at[b, k - 1], e.o_ss.at[b, k], e.o_sr.at[b, k], (s, q)))
+        for k in range(1, pairs):
+            q = wrap(n + 2 * k, nn)
+            found.append(
+                remote(e.o_pair.at[b, q // 2], e.o_sum.at[b, k - 1], e.o_ss.at[b, k], e.o_sr.at[b, k], (s, q))
+            )
         return found
 
     def near(e, b):
@@ -918,6 +957,20 @@
 
     def begin(b):
         def stage(e):
+            for copy in mates(e, b):
+                copy.start()
+
+        return stage
+
+    def pair(b):
+        def stage(e):
+            s, n = place()
+            for copy in mates(e, b):
+                copy.wait()
+            for k in range(pairs):
+                q = lax.rem(n, 2) + 2 * k
+                rows = pl.ds(pl.multiple_of(q * L, 16), L)
+                e.o_pair[b, k] = (e.o_rows[b, rows].astype(F32) + e.o_half[b, k].astype(F32)).astype(BF)
             for copy in sums(e, b):
                 copy.start()
 
@@ -928,8 +981,8 @@
             s, n = place()
             for copy in sums(e, b):
                 copy.wait()
-            total = e.o_rows[b, pl.ds(pl.multiple_of(n * L, 16), L)].astype(F32)
-            for k in range(1, nn):
+            total = e.o_pair[b, n // 2].astype(F32)
+            for k in range(1, pairs):
                 total = total + e.o_sum[b, k - 1].astype(F32)
             turned = total.T
             e.o_send[b] = turned.astype(BF)
@@ -962,18 +1015,23 @@
 
     return SimpleNamespace(
         begin=begin,
+        pair=pair,
         middle=middle,
         finish=finish,
         ins={},
         outs=dict(o_grad=out((B, R, L), F32)),
         scr=dict(
-            o_sum=pltpu.VMEM((B, nn - 1, L, TP), BF),
+            o_half=pltpu.VMEM((B, pairs, L, TP), BF),
+            o_pair=pltpu.VMEM((B, pairs, L, TP), BF),
+            o_sum=pltpu.VMEM((B, pairs - 1, L, TP), BF),
+            o_hs=dma(B, pairs),
+            o_hr=dma(B, pairs),
             o_send=pltpu.VMEM((B, TP, L), BF),
             o_near=pltpu.VMEM((B, 2, R, L), BF),
             o_fsend=pltpu.VMEM((B, FAR, L), F32),
             o_frecv=pltpu.VMEM((B, FAR, L), F32),
-            o_ss=dma(B, nn),
-            o_sr=dma(B, nn),
+            o_ss=dma(B, pairs),
+            o_sr=dma(B, pairs),
             o_ns=dma(B, 2),
             o_nr=dma(B, 2),
             o_fs=dma(B, ns),
@@ -982,11 +1040,12 @@
     )
 
 
-def cut(z, total, start):
+def cut(total, start, rounds):
     unit = 16 << SPLITS
-    units = max(3, -(-total // unit))
-    sizes = [units // 3 + (1 if k < units % 3 else 0) for k in range(3)]
-    starts = [start + sum(sizes[:k]) * unit for k in range(3)]
+    units = max(3 * rounds, -(-total // unit))
+    count = 3 * rounds
+    sizes = [units // count + (1 if k < units % count else 0) for k in range(count)]
+    starts = [start + sum(sizes[:k]) * unit for k in range(count)]
     return start + units * unit, [(at, size * unit) for at, size in zip(starts, sizes)]
 
 
@@ -1008,12 +1067,13 @@
             setattr(at, name, row)
             row += size
         used = row
-        row, parts = cut(z, used - first, first)
+        row, parts = cut(used - first, first, ROUNDS if group is early else 1)
         if group is early:
             at.early, at.early_end = parts, used
         else:
             at.late, at.late_end = parts, used
-    at.rows = row
+    at.span = row
+    at.rows = -(-row // (2 * DN)) * 2 * DN
     at.middle = at.late[0][0]
     return at
 
@@ -1024,7 +1084,8 @@
     phases = len(orders[0])
     most = max(size for _, size in at.early + at.late) >> phases
     parts = at.early + at.late
-    groups = (range(3), range(3, 6))
+    groups = [range(k, k + 3) for k in range(0, len(parts), 3)]
+    count = len(parts)
 
     def bit_value(axis, bit):
         s, n = place()
@@ -1148,7 +1209,7 @@
         put(e, at.own, side([e.p_dwn[...], gap, e.p_dwo[...], gap]))
         narrow = side([e.p_vec[...], jnp.zeros((8, DN - DE), F32)])
         put(e, at.vec, jnp.concatenate([e.p_vec0[...] + e.b_ovec[...], narrow, e.g_vec[...]], 0))
-        clear(e, at.late_end, at.rows)
+        clear(e, at.late_end, at.span)
 
     f0, f1, b0, ee = early
     return SimpleNamespace(
@@ -1179,55 +1240,109 @@
         ),
         outs=dict(s_out=(jax.ShapeDtypeStruct((at.rows, DN), BF), pl.BlockSpec(memory_space=pl.ANY))),
         scr=dict(
-            s_buf=pltpu.VMEM((at.rows, DN), BF),
-            s_recv=pltpu.VMEM((at.rows, DN), BF),
-            s_os=dma(6),
-            s_more=pltpu.VMEM((6, len(whole), most, DN) if whole else (16, DN), BF),
-            s_ms=dma(6, max(1, len(whole))),
-            s_mr=dma(6, max(1, len(whole))),
-            s_ds=dma(6, phases),
-            s_dr=dma(6, phases),
-            s_us=dma(6, phases),
-            s_ur=dma(6, phases),
-        ),
-    )
-
-
-def unpack_kernel(z, packed, at):
-    DN, DE, FF = z.DN, z.DE, z.FF
-
-    def kernel(p, ws, wp, we, wo, wi, wf, es, ep, own, eo, *vectors):
-        def get(row, size):
-            return p[row : row + size].astype(F32)
-
-        ws[...] = get(at.ws, DN)
-        wp[...] = get(at.wp, DN)
-        we[...] = get(at.we, DE)
-        wo[...] = get(at.wo, DN)
-        for k in range(FF // DN):
-            wi[:, k * DN : (k + 1) * DN] = get(at.wi + k * DN, DN)
-        wf[...] = get(at.wf, FF)
-        es[...] = get(at.es, DE)
-        ep[...] = get(at.ep, DE)
-        pair = get(at.own, DE)
-        own[...] = pair[:, :DE]
-        eo[...] = pair[:, 256 : 256 + DE]
-        vec = get(at.vec, 32)
-        hidden = side([vec[6 + k : 7 + k] for k in range(FF // DN)])
-        vectors[0][...] = hidden.reshape(FF)
-        for ref, row in zip(vectors[1:], (24, 0, 1, 2, 3, 4, 5, 16, 17, 18, 19), strict=True):
-            wide = ref.shape[0]
-            ref[...] = vec[row : row + 1, :wide].reshape(wide)
+            s_buf=pltpu.VMEM((at.span, DN), BF),
+            s_recv=pltpu.VMEM((at.span, DN), BF),
+            s_os=dma(count),
+            s_more=pltpu.VMEM((count, len(whole), most, DN) if whole else (16, DN), BF),
+            s_ms=dma(count, max(1, len(whole))),
+            s_mr=dma(count, max(1, len(whole))),
+            s_ds=dma(count, phases),
+            s_dr=dma(count, phases),
+            s_us=dma(count, phases),
+            s_ur=dma(count, phases),
+        ),
+    )
+
+
+def unpack_kernel(z, packed, at, edge, final, node, fresh):
+    DN, DE, FF, B, S, R = z.DN, z.DE, z.FF, z.B, z.S, z.R
+    size, wide = 2 * DN, FF // DN
+    half = wide // 2
+    steps = at.rows // size
+    slots = S // 3
+    blocks = B * 3
+
+    def kernel(p, *refs):
+        given, (ws, wp, we, wo, wi, wf, es, ep, own, eo, *vectors), rest = refs[: B + 3], refs[B + 3 : B + 25], refs[B + 25 :]
+        step = pl.program_id(0)
+
+        @pl.when(step < blocks)
+        def _():
+            rest[0][...] = given[0][...]
+            rest[1][...] = given[1][...]
+
+        @pl.when(step == 0)
+        def _():
+            rest[2][...] = given[2][...]
+            for b in range(B):
+                rest[3][b] = given[3 + b][...]
+
+        def take(row, count):
+            return p[row % size : row % size + count].astype(F32)
+
+        def at_row(row):
+            return pl.when(step == row // size)
+
+        @pl.when(step < half)
+        def _():
+            wi[:, :DN] = p[:DN].astype(F32)
+            wi[:, DN:] = p[DN:].astype(F32)
+
+        @pl.when(jnp.logical_and(step >= half, step < 2 * half))
+        def _():
+            wf[...] = p[...].astype(F32)
+
+        @at_row(at.wo)
+        def _():
+            wo[...] = take(at.wo, DN)
+
+        @at_row(at.es)
+        def _():
+            es[...] = take(at.es, DE)
+            ep[...] = take(at.ep, DE)
+
+        @at_row(at.ws)
+        def _():
+            ws[...] = take(at.ws, DN)
+
+        @at_row(at.wp)
+        def _():
+            wp[...] = take(at.wp, DN)
+
+        @at_row(at.we)
+        def _():
+            we[...] = take(at.we, DE)
+            both = take(at.own, DE)
+            own[...] = both[:, :DE]
+            eo[...] = both[:, 256 : 256 + DE]
+            vec = take(at.vec, 32)
+            vectors[0][...] = side([vec[6 + k : 7 + k] for k in range(wide)]).reshape(FF)
+            for ref, row in zip(vectors[1:], (24, 0, 1, 2, 3, 4, 5, 16, 17, 18, 19), strict=True):
+                count = ref.shape[0]
+                ref[...] = vec[row : row + 1, :count].reshape(count)
 
     shapes = [(DN, DN), (DN, DN), (DE, DN), (DN, DN), (DN, FF), (FF, DN), (DE, DN), (DE, DN), (DE, DE), (DE, DE)]
     shapes += [(FF,)] + [(DN,)] * 7 + [(DE,)] * 4
+    here = pl.BlockSpec(memory_space=pltpu.VMEM)
+    specs = [here] * len(shapes)
+    specs[4] = pl.BlockSpec((DN, size), lambda i: (0, jnp.clip(i, 0, half - 1)))
+    specs[5] = pl.BlockSpec((size, DN), lambda i: (jnp.clip(i - half, 0, half - 1), 0))
+
+    def turn(i):
+        k = jnp.minimum(i, blocks - 1)
+        return (k // 3, lax.rem(k, 3), 0, 0)
+
+    stream = pl.BlockSpec((1, slots, DE, R), turn)
     return pl.pallas_call(
         kernel,
-        out_shape=[jax.ShapeDtypeStruct(shape, F32) for shape in shapes],
-        in_specs=[pl.BlockSpec(memory_space=pltpu.VMEM)],
-        out_specs=[pl.BlockSpec(memory_space=pltpu.VMEM)] * len(shapes),
+        grid=(steps,),
+        out_shape=[jax.ShapeDtypeStruct(shape, F32) for shape in shapes]
+        + [jax.ShapeDtypeStruct(x.shape, x.dtype) for x in (edge, final, node)]
+        + [jax.ShapeDtypeStruct((B,) + fresh[0].shape, fresh[0].dtype)],
+        in_specs=[pl.BlockSpec((size, DN), lambda i: (i, 0)), stream, stream, here] + [here] * B,
+        out_specs=specs + [stream, stream, here, here],
         compiler_params=pltpu.CompilerParams(vmem_limit_bytes=VMEM_LIMIT),
-    )(packed)
+    )(packed, edge, final, node, *fresh)
 
 
 def local(
@@ -1282,6 +1397,7 @@
     def plain(part):
         return SimpleNamespace(ins=part, outs={}, scr={})
 
+    heavy = ("w_in", "w_ffn")
     small, table, message = setup_part(z, a), table_part(z, a), message_part(z, a)
     node0 = forward_part(z, a, 0, lambda e: e.part_a)
     f0 = build(
@@ -1293,10 +1409,11 @@
         {
             1: [table.middle(1)],
             3: [table.finish(1)],
-            T + 1: [node0.compute],
+            T + 1: [ready, node0.compute],
             T + 3: [node0.spread],
             2 * T - 1: [node0.finish],
         },
+        heavy,
     )
     shared = plain(dict(vecs=vm(f0.vecs), send=vm(f0.send)))
 
@@ -1310,13 +1427,14 @@
         2 * T,
         {0: [node1.begin], T: [back0.begin]},
         {
-            1: [node1.compute],
+            1: [ready, node1.compute],
             3: [node1.spread],
             T - 1: [node1.finish],
             T + 1: [back0.gather],
             T + 2: [back0.compute],
             2 * T - 1: [back0.finish],
         },
+        heavy,
     )
 
     at = pack_rows(z)
@@ -1327,24 +1445,32 @@
     for name, (shape, spec) in back1.outs.items():
         back1.scr[name] = pltpu.VMEM(shape.shape, shape.dtype)
     back1.outs = {}
-    D = total.phases
-    tail = [outer.begin(1), total.pack_late, total.begin(1), total.fold(0, D - 1)]
-    tail += [total.fold(1, 0), outer.middle(1)]
+    D, late = total.phases, ROUNDS
+
+    def fold(d):
+        return [total.fold(k, d) for k in range(ROUNDS)]
+
+    def gather(d):
+        return [total.spread(k, d) for k in range(ROUNDS)]
+
+    tail = [outer.begin(1), total.pack_late, total.begin(late)] + fold(D - 1) + [outer.pair(1)]
+    tail += [total.fold(late, 0), outer.middle(1)]
     for d in reversed(range(D)):
-        tail.append(total.spread(0, d))
-        if D - d < D:
-            tail.append(total.fold(1, D - d))
+        tail += gather(d)
+        if d:
+            tail.append(total.fold(late, D - d))
         if d == D - 3:
-            tail.append(outer.finish(1))
-    tail += [total.spread(1, d) for d in reversed(range(D))]
+            tail += [outer.finish(0), outer.finish(1)]
+    tail += [total.spread(late, d) for d in reversed(range(D))]
     after = {
         1: [back1.gather],
-        2: [back1.compute, total.pack_early, total.begin(0)],
-        3: [total.fold(0, 0)],
+        2: [ready, back1.compute, total.pack_early] + [total.begin(k) for k in range(ROUNDS)],
+        3: fold(0),
         T - 1: [back1.finish],
-        T + 1: [total.fold(0, 1)],
-        T + 2: [outer.middle(0), total.fold(0, 2)],
-        2 * T - 1: [outer.finish(0)] + [total.fold(0, d) for d in range(3, D - 1)] + tail,
+        T: [outer.pair(0)] + fold(1),
+        T + 1: fold(2),
+        T + 2: [outer.middle(0)] + fold(3),
+        2 * T - 1: tail,
     }
     grads = dict(e_tgrad=vm(f1.e_tgrad), e_fgrad=vm(f1.e_fgrad), e_sgrad=vm(f1.e_sgrad))
     f2 = build(
@@ -1354,14 +1480,17 @@
         2 * T,
         {0: [back1.begin], T: [outer.begin(0)]},
         after,
-    )
-    ws, wp, we, wo, wi, wf, es, ep, own, eo, *vectors = unpack_kernel(z, f2.s_out, at)
-    hidden, mb, ms, fg, fs, ob, sg, ss, eb, esh, tg, ts = vectors
+        heavy + ("p_act0", "p_act1", "p_ffn0"),
+    )
+    ws, wp, we, wo, wi, wf, es, ep, own, eo, *vectors = unpack_kernel(
+        z, f2.s_out, at, f2.g_edge, f1.e_final, f2.o_grad, [f0.f_onew, f1.f_onew]
+    )
+    hidden, mb, ms, fg, fs, ob, sg, ss, eb, esh, tg, ts, edge_grad, new_edges, node_grad, new_nodes = vectors
     return (
-        jnp.stack([f0.f_onew, f1.f_onew]),
-        f1.e_final.transpose(0, 3, 1, 2),
-        f2.o_grad,
-        f2.g_edge.transpose(0, 3, 1, 2),
+        new_nodes,
+        new_edges.transpose(0, 3, 1, 2),
+        node_grad,
+        edge_grad.transpose(0, 3, 1, 2),
         ws,
         wp,
         we,

time: 286 us -> 270 us (0.944)
  local copies, waits for them, and re-layouts: 7.81 us -> 0 us
  Pallas kernels: 276 us -> 269 us
    pallas_call x3, Pallas kernels: 268 us -> 252 us  [build(): pl.pallas_call(kernel, grid=(steps,), out_shape=[shape for shape, _ in ou...]
    pallas_call x1, Pallas kernels: 7.84 us -> 16.6 us  [unpack_kernel(): pl.pallas_call(kernel, grid=(steps,), out_shape=[jax.ShapeDtypeStruct(sha...]
    unnamed x11 -> x0, local copies, waits for them, and re-layouts: 7.81 us -> none
where the time goes in v2:
time: 270 us
  Pallas kernels  269 us (100%)
    pallas_call x3, Pallas kernels, build(): pl.pallas_call(kernel, grid=(steps,), out_shape=[shape for shape, _ in ou...  252 us
    pallas_call x1, Pallas kernels, unpack_kernel(): pl.pallas_call(kernel, grid=(steps,), out_shape=[jax.ShapeDtypeStruct(sha...  16.6 us

profile of v2, /device:TPU:0, one launch (start us, length us, event | category | flops | bytes accessed | tf_op | source)
XLA Modules:
  0.0 269.8 jit_solution(4746258862476969819)
XLA Ops:
  0.7 65.7 %shard_map.476 = (f32[24,512]{1,0:T(8,128)}, s32[2,1,64]{2,1,0:T(1,128)}, bf16[2,1280,512]{2,1,0:T(8,128)(2,1)}, bf16[2,15,512,384]{3,2,1,0:T(8,128)(2,1)}, bf16...) custom-call(bf16[512]{0:T(512)(128)(2,1)} %refs_0_.1, ...), custom_call_target="tpu_custom_call" | custom-call | tf_op jit(solution)/shard_map/pallas_call | solution.py:146
  66.4 60.3 %shard_map.477 = (bf16[2,15,192,384]{3,2,1,0:T(8,128)(2,1)}, bf16[2,15,192,384]{3,2,1,0:T(8,128)(2,1)}, bf16[1280,192]{1,0:T(8,128)(2,1)}, f32[64,192]{1,0:T(8,1...) custom-call(f32[24,512]{1,0:T(8,128)} %get-tuple-element.98.refs_0_,, ...), custom_call_target="tpu_custom_call" | custom-call | tf_op jit(solution)/shard_map/pallas_call | solution.py:146
  126.6 126.4 %shard_map.478 = (bf16[2,15,192,384]{3,2,1,0:T(8,128)(2,1)}, f32[2,384,128]{2,1,0:T(8,128)}, bf16[7168,512]{1,0:T(8,128)(2,1)}) custom-call(f32[24,512]{1,0:T(8,128)} %get-tuple-element.98.refs_0_, s32[2,1,64]{2,1,0:T(1,128)} %get-tuple-element.99.refs_1_, bf16[1280,192]{1,0:T(8,128)(2,1)} %get-tuple-element.109.refs_2_, ...), custom_call_target="tpu_custom_call" | custom-call | tf_op jit(solution)/shard_map/pallas_call | solution.py:146
  253.0 16.6 %shard_map.479 = (f32[512,512]{1,0:T(8,128)}, f32[512,512]{1,0:T(8,128)}, f32[192,512]{1,0:T(8,128)}, f32[512,512]{1,0:T(8,128)}, f32[512,2048]{1,0:T(8,128)}, /...) custom-call(bf16[7168,512]{1,0:T(8,128)(2,1)} %get-tuple-element.139, ...), custom_call_target="tpu_custom_call" | custom-call | tf_op jit(solution)/shard_map/pallas_call | solution.py:1336

commit v3 on v2

--- a/solution.py
+++ b/solution.py
@@ -286,10 +286,15 @@
             found.append(remote(rows, rows, e.t_ms.at[b, k], e.t_mr.at[b, k], (s, flip(n, 0))))
         return found
 
-    def begin(b):
+    def launch(b):
         def stage(e):
             for copy in near(e, b):
                 copy.start()
+
+        return stage
+
+    def begin(b):
+        def stage(e):
             own = e.nodes[b]
             e.t_fsend[b] = dot_tn(hot(e.send[b], R), own)
             for copy in far(e, b):
@@ -323,6 +328,7 @@
         return stage
 
     return SimpleNamespace(
+        launch=launch,
         begin=begin,
         middle=middle,
         finish=finish,
@@ -349,16 +355,10 @@
     def body(e, step):
         sample, own = step // T, lax.rem(step, T)
 
-        @pl.when(step == 0)
-        def _():
-            e.m_wst[...] = e.w_self[...].T
-            e.m_wpt[...] = e.w_peer[...].T
-            e.m_wet[...] = e.w_edge[...].T
-
         @pl.when(own == 0)
         def _():
             e.m_tabt[...] = dot_nt(e.m_wpt[...], e.t_tab[sample]).astype(BF)
-            e.m_selft[...] = dot_nt(e.m_wst[...], e.nodes[sample]) + e.vecs[0:8].T[:, 0:1]
+            e.m_selft[...] = e.m_selfs[sample]
             e.m_acc[...] = jnp.zeros_like(e.m_acc)
 
         slots = [own * GROUP + g for g in range(GROUP)]
@@ -382,8 +382,16 @@
             def _(ref=ref):
                 ref[...] = e.m_acc[...].T.astype(BF)
 
+    def prepare(e):
+        e.m_wpt[...] = e.w_peer[...].T
+        e.m_wet[...] = e.w_edge[...].T
+        turned = e.w_self[...].T
+        for b in range(B):
+            e.m_selfs[b] = dot_nt(turned, e.nodes[b]) + e.vecs[0:8].T[:, 0:1]
+
     return SimpleNamespace(
         body=body,
+        prepare=prepare,
         ins=dict(
             nodes=vm(a.nodes),
             m_edges=(a.edges_t, pl.BlockSpec((1, GROUP, DE, R), lambda i: (i // T, lax.rem(i, T), 0, 0))),
@@ -404,7 +412,7 @@
             part_a=pltpu.VMEM((R, DN + LANES), BF),
             m_tabt=pltpu.VMEM((DN, TP), BF),
             m_selft=pltpu.VMEM((DN, R), F32),
-            m_wst=pltpu.VMEM((DN, DN), BF),
+            m_selfs=pltpu.VMEM((B, DN, R), F32),
             m_wpt=pltpu.VMEM((DN, DN), BF),
             m_wet=pltpu.VMEM((DN, DE), BF),
             m_acc=pltpu.VMEM((DN + LANES, R), F32),
@@ -831,13 +839,13 @@
     T = S // GROUP
 
     def body(e, step):
-        sample, own = step // T, lax.rem(step, T)
+        sample, own = lax.rem(step // T, B), lax.rem(step, T)
         for b, ref in enumerate((e.a_all, e.b_all)):
 
             @pl.when(step == b * T)
             def _(ref=ref, b=b):
                 pltpu.make_async_copy(e.g_tables.at[b], e.g_tab, e.g_ts.at[b]).start()
-                e.g_ht[...] = dot_nt(e.w_out[...], ref[:, 0:DN])
+                e.g_ht[b] = dot_nt(e.w_out[...], ref[:, 0:DN])
                 e.g_ptab[...] = jnp.zeros_like(e.g_ptab)
                 e.g_sacc[...] = jnp.zeros_like(e.g_sacc)
                 if b == 0:
@@ -846,48 +854,69 @@
 
         line = pl.ds(sample, 1)
         slots = [own * GROUP + g for g in range(GROUP)]
-        index = hot(side([e.nbr[s, line] for s in slots]), TP)
-        edge = side([e.m_edges[0, g] for g in range(GROUP)])
-        inner = []
-        acc = e.g_sacc[...]
-        for g, s in enumerate(slots):
-            piece = (e.g_slope[0, g].astype(F32) * (e.g_ht[...] * e.live[s, line].astype(F32))).astype(BF)
-            acc = acc + piece.astype(F32)
-            inner.append(piece)
-        e.g_sacc[...] = acc
-        inner = side(inner)
-        e.g_ptab[...] += dot_nt(inner, index)
-        e.g_dwe[...] += dot_nt(edge, inner)
-        back = dot(e.w_edge[...], inner)
-        for g in range(GROUP):
-            e.g_edge[0, g] = (back[:, g * R : (g + 1) * R] + e.g_part[0, g].astype(F32)).astype(BF)
+
+        def pieces():
+            return [
+                (e.g_slope[0, g].astype(F32) * (e.g_ht[sample] * e.live[s, line].astype(F32))).astype(BF)
+                for g, s in enumerate(slots)
+            ]
+
+        @pl.when(step < B * T)
+        def _():
+            index = hot(side([e.nbr[s, line] for s in slots]), TP)
+            edge = side([e.m_edges[0, g] for g in range(GROUP)])
+            inner = pieces()
+            acc = e.g_sacc[...]
+            for piece in inner:
+                acc = acc + piece.astype(F32)
+            e.g_sacc[...] = acc
+            inner = side(inner)
+            e.g_ptab[...] += dot_nt(inner, index)
+            e.g_dwe[...] += dot_nt(inner, edge)
+
+        @pl.when(step >= B * T)
+        def _():
+            back = dot(e.w_edge[...], side(pieces()))
+            for g in range(GROUP):
+                e.g_edge[0, g] = (back[:, g * R : (g + 1) * R] + e.g_part[0, g].astype(F32)).astype(BF)
+
         for b in range(B):
 
             @pl.when(step == (b + 1) * T - 1)
             def _(b=b):
                 self_t = e.g_sacc[...].astype(BF)
                 peer_t = e.g_ptab[...].astype(BF)
+                e.o_rows[b] = dot(e.w_peer[...], peer_t).astype(BF)
+                e.o_rows[b, :, R : 2 * R] = (
+                    dot(e.w_peer[...], peer_t[:, R : 2 * R]) + dot(e.w_self[...], self_t)
+                ).astype(BF)
                 pltpu.make_async_copy(e.g_tables.at[b], e.g_tab, e.g_ts.at[b]).wait()
                 dself = dot(self_t, e.nodes[b])
                 dpeer = dot(peer_t, e.g_tab[...])
                 e.g_dself[...] = dself if b == 0 else e.g_dself[...] + dself
                 e.g_dpeer[...] = dpeer if b == 0 else e.g_dpeer[...] + dpeer
                 e.g_vec[0:1] += row_sum(e.g_sacc[...].T)
-                e.o_rows[b] = dot(e.w_peer[...], peer_t).astype(BF)
-                e.o_rows[b, :, R : 2 * R] = (
-                    dot(e.w_peer[...], peer_t[:, R : 2 * R]) + dot(e.w_self[...], self_t)
-                ).astype(BF)
-
-    stream = pl.BlockSpec((1, GROUP, DE, R), lambda i: (i // T, lax.rem(i, T), 0, 0))
+
+    def always(i):
+        return (lax.rem(i // T, B), lax.rem(i, T), 0, 0)
+
+    def early(i):
+        k = jnp.minimum(i, B * T - 1)
+        return (k // T, lax.rem(k, T), 0, 0)
+
+    def late(i):
+        k = jnp.maximum(i - B * T, 0)
+        return (k // T, lax.rem(k, T), 0, 0)
+
     return SimpleNamespace(
         body=body,
         ins=dict(
             a_all=vm(spread),
-            g_slope=(slope, pl.BlockSpec((1, GROUP, DN, R), lambda i: (i // T, lax.rem(i, T), 0, 0))),
-            g_part=(part, stream),
+            g_slope=(slope, pl.BlockSpec((1, GROUP, DN, R), always)),
+            g_part=(part, pl.BlockSpec((1, GROUP, DE, R), late)),
             g_tables=(tables, pl.BlockSpec(memory_space=pl.ANY)),
             nodes=vm(a.nodes),
-            m_edges=(a.edges_t, stream),
+            m_edges=(a.edges_t, pl.BlockSpec((1, GROUP, DE, R), early)),
             nbr=vm(a.nbr),
             live=vm(a.live),
             w_self=vm(a.message_self),
@@ -895,16 +924,16 @@
             w_edge=vm(a.message_edge),
             w_out=vm(a.message_out),
         ),
-        outs=dict(g_edge=(jax.ShapeDtypeStruct((B, S, DE, R), BF), stream)),
+        outs=dict(g_edge=(jax.ShapeDtypeStruct((B, S, DE, R), BF), pl.BlockSpec((1, GROUP, DE, R), late))),
         scr=dict(
             g_tab=pltpu.VMEM((TP, DN), BF),
             g_ts=dma(B),
-            g_ht=pltpu.VMEM((DN, R), F32),
+            g_ht=pltpu.VMEM((B, DN, R), F32),
             g_ptab=pltpu.VMEM((DN, TP), F32),
             g_sacc=pltpu.VMEM((DN, R), F32),
             g_dself=pltpu.VMEM((DN, DN), F32),
             g_dpeer=pltpu.VMEM((DN, DN), F32),
-            g_dwe=pltpu.VMEM((DE, DN), F32),
+            g_dwe=pltpu.VMEM((DN, DE), F32),
             g_vec=pltpu.VMEM((8, DN), F32),
             o_rows=pltpu.VMEM((B, DN, TP), BF),
         ),
@@ -1204,7 +1233,7 @@
     def pack_late(e):
         put(e, at.ws, e.g_dself[...].T)
         put(e, at.wp, e.g_dpeer[...].T)
-        put(e, at.we, e.g_dwe[...])
+        put(e, at.we, e.g_dwe[...].T)
         gap = jnp.zeros((DE, 256 - DE), F32)
         put(e, at.own, side([e.p_dwn[...], gap, e.p_dwo[...], gap]))
         narrow = side([e.p_vec[...], jnp.zeros((8, DN - DE), F32)])
@@ -1405,7 +1434,19 @@
         [small, table, message, node0],
         lambda: near_cross(z) + same_lane(z),
         2 * T,
-        {0: [small.begin, table.begin(0), table.middle(0), table.begin(1), table.finish(0)], T: [node0.begin]},
+        {
+            0: [
+                table.launch(0),
+                small.begin,
+                table.begin(0),
+                message.prepare,
+                table.middle(0),
+                table.launch(1),
+                table.begin(1),
+                table.finish(0),
+            ],
+            T: [node0.begin],
+        },
         {
             1: [table.middle(1)],
             3: [table.finish(1)],
@@ -1453,31 +1494,35 @@
     def gather(d):
         return [total.spread(k, d) for k in range(ROUNDS)]
 
-    tail = [outer.begin(1), total.pack_late, total.begin(late)] + fold(D - 1) + [outer.pair(1)]
-    tail += [total.fold(late, 0), outer.middle(1)]
-    for d in reversed(range(D)):
-        tail += gather(d)
-        if d:
-            tail.append(total.fold(late, D - d))
-        if d == D - 3:
-            tail += [outer.finish(0), outer.finish(1)]
-    tail += [total.spread(late, d) for d in reversed(range(D))]
+    lf, ls = (lambda d: total.fold(late, d)), (lambda d: total.spread(late, d))
+    f, g = total.fold, total.spread
     after = {
         1: [back1.gather],
         2: [ready, back1.compute, total.pack_early] + [total.begin(k) for k in range(ROUNDS)],
-        3: fold(0),
-        T - 1: [back1.finish],
-        T: [outer.pair(0)] + fold(1),
-        T + 1: fold(2),
-        T + 2: [outer.middle(0)] + fold(3),
-        2 * T - 1: tail,
+        3: [f(0, 0)],
+        T - 1: [back1.finish, f(1, 0)],
+        T: [f(0, 1)],
+        T + 1: [outer.pair(0), f(1, 1)],
+        T + 2: [f(0, 2)],
+        T + 3: [f(1, 2)],
+        2 * T - 1: [f(0, 3), outer.middle(0), outer.begin(1), total.pack_late, total.begin(late)],
+        2 * T: [f(1, 3), lf(0)],
+        2 * T + 1: [f(0, 4), outer.pair(1)],
+        2 * T + 2: [lf(1), f(1, 4)],
+        2 * T + 3: [lf(2), g(0, 4)],
+        2 * T + 4: [outer.middle(1), lf(3)],
+        3 * T: [g(1, 4), lf(4)],
+        3 * T + 1: [g(0, 3)],
+        3 * T + 2: [ls(4), g(1, 3)],
+        3 * T + 3: [g(0, 2), ls(3)],
+        4 * T - 1: [g(1, 2), ls(2), g(0, 1), ls(1), outer.finish(0), g(1, 1), ls(0), g(0, 0), outer.finish(1), g(1, 0)],
     }
     grads = dict(e_tgrad=vm(f1.e_tgrad), e_fgrad=vm(f1.e_fgrad), e_sgrad=vm(f1.e_sgrad))
     f2 = build(
         ids,
         [shared, plain(grads), last, back1, outer, total],
         lambda: [(lax.axis_index("space"), wrap(lax.axis_index("nbr") + k, nn)) for k in range(1, nn)] + same_lane(z),
-        2 * T,
+        4 * T,
         {0: [back1.begin], T: [outer.begin(0)]},
         after,
         heavy + ("p_act0", "p_act1", "p_ffn0"),

time: 270 us -> 257 us (0.952)
  Pallas kernels: 269 us -> 256 us
    pallas_call x3, Pallas kernels: 252 us -> 240 us  [build(): pl.pallas_call(kernel, grid=(steps,), out_shape=[shape for shape, _ in ou...]
where the time goes in v3:
time: 257 us
  Pallas kernels  256 us (100%)
    pallas_call x3, Pallas kernels, build(): pl.pallas_call(kernel, grid=(steps,), out_shape=[shape for shape, _ in ou...  240 us
    pallas_call x1, Pallas kernels, unpack_kernel(): pl.pallas_call(kernel, grid=(steps,), out_shape=[jax.ShapeDtypeStruct(sha...  16.6 us

profile of v3, /device:TPU:0, one launch (start us, length us, event | category | flops | bytes accessed | tf_op | source)
XLA Modules:
  0.0 257.0 jit_solution(16238346484768535974)
XLA Ops:
  0.7 64.9 %shard_map.476 = (f32[24,512]{1,0:T(8,128)}, s32[2,1,64]{2,1,0:T(1,128)}, bf16[2,1280,512]{2,1,0:T(8,128)(2,1)}, bf16[2,15,512,384]{3,2,1,0:T(8,128)(2,1)}, bf16...) custom-call(bf16[512]{0:T(512)(128)(2,1)} %refs_0_.1, ...), custom_call_target="tpu_custom_call" | custom-call | tf_op jit(solution)/shard_map/pallas_call | solution.py:146
  65.6 60.3 %shard_map.477 = (bf16[2,15,192,384]{3,2,1,0:T(8,128)(2,1)}, bf16[2,15,192,384]{3,2,1,0:T(8,128)(2,1)}, bf16[1280,192]{1,0:T(8,128)(2,1)}, f32[64,192]{1,0:T(8,1...) custom-call(f32[24,512]{1,0:T(8,128)} %get-tuple-element.98.refs_0_,, ...), custom_call_target="tpu_custom_call" | custom-call | tf_op jit(solution)/shard_map/pallas_call | solution.py:146
  125.9 114.4 %shard_map.478 = (bf16[2,15,192,384]{3,2,1,0:T(8,128)(2,1)}, f32[2,384,128]{2,1,0:T(8,128)}, bf16[7168,512]{1,0:T(8,128)(2,1)}) custom-call(f32[24,512]{1,0:T(8,128)} %get-tuple-element.98.refs_0_, s32[2,1,64]{2,1,0:T(1,128)} %get-tuple-element.99.refs_1_, bf16[1280,192]{1,0:T(8,128)(2,1)} %get-tuple-element.109.refs_2_, ...), custom_call_target="tpu_custom_call" | custom-call | tf_op jit(solution)/shard_map/pallas_call | solution.py:146
  240.3 16.6 %shard_map.479 = (f32[512,512]{1,0:T(8,128)}, f32[512,512]{1,0:T(8,128)}, f32[192,512]{1,0:T(8,128)}, f32[512,512]{1,0:T(8,128)}, f32[512,2048]{1,0:T(8,128)}, /...) custom-call(bf16[7168,512]{1,0:T(8,128)(2,1)} %get-tuple-element.139, ...), custom_call_target="tpu_custom_call" | custom-call | tf_op jit(solution)/shard_map/pallas_call | solution.py:1365

commit v4 on v3

--- a/solution.py
+++ b/solution.py
@@ -1448,8 +1448,8 @@
             T: [node0.begin],
         },
         {
-            1: [table.middle(1)],
-            3: [table.finish(1)],
+            2: [table.middle(1)],
+            4: [table.finish(1)],
             T + 1: [ready, node0.compute],
             T + 3: [node0.spread],
             2 * T - 1: [node0.finish],
@@ -1471,8 +1471,8 @@
             1: [ready, node1.compute],
             3: [node1.spread],
             T - 1: [node1.finish],
-            T + 1: [back0.gather],
-            T + 2: [back0.compute],
+            T + 2: [back0.gather],
+            T + 3: [back0.compute],
             2 * T - 1: [back0.finish],
         },
         heavy,
@@ -1502,14 +1502,14 @@
         3: [f(0, 0)],
         T - 1: [back1.finish, f(1, 0)],
         T: [f(0, 1)],
-        T + 1: [outer.pair(0), f(1, 1)],
+        T + 1: [f(1, 1)],
         T + 2: [f(0, 2)],
-        T + 3: [f(1, 2)],
-        2 * T - 1: [f(0, 3), outer.middle(0), outer.begin(1), total.pack_late, total.begin(late)],
+        T + 3: [f(1, 2), outer.pair(0)],
+        2 * T - 1: [f(0, 3), outer.begin(1), total.pack_late, total.begin(late)],
         2 * T: [f(1, 3), lf(0)],
         2 * T + 1: [f(0, 4), outer.pair(1)],
         2 * T + 2: [lf(1), f(1, 4)],
-        2 * T + 3: [lf(2), g(0, 4)],
+        2 * T + 3: [outer.middle(0), lf(2), g(0, 4)],
         2 * T + 4: [outer.middle(1), lf(3)],
         3 * T: [g(1, 4), lf(4)],
         3 * T + 1: [g(0, 3)],

time: 257 us -> 251 us (0.977)
  Pallas kernels: 256 us -> 250 us
    pallas_call x3, Pallas kernels: 240 us -> 233 us  [build(): pl.pallas_call(kernel, grid=(steps,), out_shape=[shape for shape, _ in ou...]
where the time goes in v4:
time: 251 us; the launch traced here: 250 us
  Pallas kernels  250 us (100%)
    pallas_call x3, Pallas kernels, build(): pl.pallas_call(kernel, grid=(steps,), out_shape=[shape for shape, _ in ou...  233 us
    pallas_call x1, Pallas kernels, unpack_kernel(): pl.pallas_call(kernel, grid=(steps,), out_shape=[jax.ShapeDtypeStruct(sha...  16.6 us

profile of v4, /device:TPU:0, one launch (start us, length us, event | category | flops | bytes accessed | tf_op | source)
XLA Modules:
  0.0 250.4 jit_solution(2842075986574815317)
XLA Ops:
  0.7 63.8 %shard_map.476 = (f32[24,512]{1,0:T(8,128)}, s32[2,1,64]{2,1,0:T(1,128)}, bf16[2,1280,512]{2,1,0:T(8,128)(2,1)}, bf16[2,15,512,384]{3,2,1,0:T(8,128)(2,1)}, bf16...) custom-call(bf16[512]{0:T(512)(128)(2,1)} %refs_0_.1, ...), custom_call_target="tpu_custom_call" | custom-call | tf_op jit(solution)/shard_map/pallas_call | solution.py:146
  64.4 58.9 %shard_map.477 = (bf16[2,15,192,384]{3,2,1,0:T(8,128)(2,1)}, bf16[2,15,192,384]{3,2,1,0:T(8,128)(2,1)}, bf16[1280,192]{1,0:T(8,128)(2,1)}, f32[64,192]{1,0:T(8,1...) custom-call(f32[24,512]{1,0:T(8,128)} %get-tuple-element.98.refs_0_,, ...), custom_call_target="tpu_custom_call" | custom-call | tf_op jit(solution)/shard_map/pallas_call | solution.py:146
  123.3 110.3 %shard_map.478 = (bf16[2,15,192,384]{3,2,1,0:T(8,128)(2,1)}, f32[2,384,128]{2,1,0:T(8,128)}, bf16[7168,512]{1,0:T(8,128)(2,1)}) custom-call(f32[24,512]{1,0:T(8,128)} %get-tuple-element.98.refs_0_, s32[2,1,64]{2,1,0:T(1,128)} %get-tuple-element.99.refs_1_, bf16[1280,192]{1,0:T(8,128)(2,1)} %get-tuple-element.109.refs_2_, ...), custom_call_target="tpu_custom_call" | custom-call | tf_op jit(solution)/shard_map/pallas_call | solution.py:146
  233.7 16.6 %shard_map.479 = (f32[512,512]{1,0:T(8,128)}, f32[512,512]{1,0:T(8,128)}, f32[192,512]{1,0:T(8,128)}, f32[512,512]{1,0:T(8,128)}, f32[512,2048]{1,0:T(8,128)}, /...) custom-call(bf16[7168,512]{1,0:T(8,128)(2,1)} %get-tuple-element.139, ...), custom_call_target="tpu_custom_call" | custom-call | tf_op jit(solution)/shard_map/pallas_call | solution.py:1365
